TPU v7x, 128 devices: a whole 4x4x4 slice. The times are simulated.
128 devices in a mesh: ep: 16 (over x, z), sp: 8 (over y, core).
Axes of the slice: x: 4, y: 4, z: 4, core: 2. Of those that a mesh axis runs over, the one named last changes fastest.
Arguments:
- tokens: bfloat16 [16384, 3584], P(('ep', 'sp')), may hold values from -40 to 40
- cotangent: bfloat16 [16384, 3584], P(('ep', 'sp')), may hold values from -11 to 11
- norm_gain: float32 [3584], replicated, may hold values from 0.1 to 1.9
- router: float32 [3584, 16], replicated, may hold values from -0.09375 to 0.09375
- dense_gate: bfloat16 [3584, 2432], P(None, 'sp'), may hold values from -0.09375 to 0.09375
- dense_up: bfloat16 [3584, 2432], P(None, 'sp'), may hold values from -0.09375 to 0.09375
- dense_down: bfloat16 [2432, 3584], P('sp'), may hold values from -0.125 to 0.125
- expert_gate: bfloat16 [16, 3584, 2432], P('ep', None, 'sp'), may hold values from -0.09375 to 0.09375
- expert_up: bfloat16 [16, 3584, 2432], P('ep', None, 'sp'), may hold values from -0.09375 to 0.09375
- expert_down: bfloat16 [16, 2432, 3584], P('ep', 'sp'), may hold values from -0.125 to 0.125
- routes: int32 [16384, 2], P(('ep', 'sp')), may hold values from 0 to 15, all different within a row; in each aligned block of 128 rows (0 to 127, 128 to 255, ...) at most 20 rows name the same one
Outputs:
- input_grad: bfloat16 [16384, 3584], P(('ep', 'sp'))
- gain_grad: float32 [3584], replicated
- router_grad: float32 [3584, 16], replicated
Inputs may be any that keep to these rules, and one draw needn't show every extreme that they name: `routes`: each token names two different experts. Among the rows of one device no expert is named more than 20 times, and in some devices one expert is named exactly 20 times.
All inputs are finite; a program needn't handle non-finite values.
Results may differ from a plain program's by a relative error of at most 0.013.
Values may be sent and summed in bfloat16 or wider, within the bound.
No kernel may reach another device: no remote copies, remote signals or barrier semaphores. Data moves between devices by JAX's collectives and lax.ppermute only.
A program may use at most 256 MiB of HBM per device.

v0:
```python
import jax
import jax.numpy as jnp
from jax import lax
from jax.experimental import pallas as pl
from jax.experimental.pallas import tpu as pltpu
from jax.sharding import Mesh, PartitionSpec as P

EPS = 1e-05
BF = jnp.bfloat16
F32 = jnp.float32
HIGHEST = lax.Precision.HIGHEST
PEERS = 4
VMEM_LIMIT = 50 * 1024 * 1024
TRANS = (((1,), (1,)), ((), ()))


def receive_from(value, k):
    return lax.ppermute(value, "y", [(i, (i - k) % PEERS) for i in range(PEERS)])


def send_to(value, k):
    return lax.ppermute(value, "y", [(i, (i + k) % PEERS) for i in range(PEERS)])


def swap(value):
    return lax.ppermute(value, "core", [(0, 1), (1, 0)])


def over(value, axes="ep"):
    return lax.all_to_all(value, axes, split_axis=0, concat_axis=0, tiled=True)


def after(value, *others):
    return lax.optimization_barrier((value,) + others)[0]


def weight_pieces(gate, up, down):
    both = [gate.T, up.T, down]
    return [piece for value in both for piece in (value, swap(value))]


def shuffle_table(cap, group):
    size = 2 * group * cap
    row = lax.broadcasted_iota(jnp.int32, (size, size), 0)
    col = lax.broadcasted_iota(jnp.int32, (size, size), 1)
    part, left = row // (group * cap), row % (group * cap)
    return (col == left // cap * (2 * cap) + part * cap + left % cap).astype(BF)


def hidden_kernel(lengths, mixed, *refs):
    count = sum(lengths)
    taken, sources = 0, []
    for length in lengths:
        sources.append(refs[taken : taken + length])
        taken += length
    pieces = refs[count : count + 6]
    refs = refs[count + 6 :]
    if mixed:
        table, table_back = refs[:2]
        refs = refs[2:]
    into, joint, weights, normed, other, both, back, grads, sems = refs
    step = pl.program_id(0)
    part, width = pieces[0].shape
    half = weights.shape[0] // 3
    copies = []
    for i in range(6):
        start = i // 2 * half + i % 2 * part
        copies.append(
            pltpu.make_async_copy(pieces[i], weights.at[pl.ds(start, part), :], sems.at[i])
        )

    @pl.when(step == 0)
    def _():
        for copy in copies[4:] + copies[:4]:
            copy.start()
        if half > 2 * part:
            for i in range(3):
                weights[i * half + 2 * part : (i + 1) * half, :] = jnp.zeros(
                    (half - 2 * part, width), BF
                )

    size = sources[0][0].shape[0] // 2
    each = normed.shape[0] // size
    for p in range(len(lengths)):

        @pl.when(step == p // each)
        def _(p=p):
            first = p % each * size
            if mixed:
                chunk = table.shape[0]
                for i in range(2 * size // chunk):
                    got = jnp.dot(
                        table[...],
                        sources[p][0][i * chunk : (i + 1) * chunk, :],
                        preferred_element_type=F32,
                    ).astype(BF)
                    at = slice(first + i * chunk // 2, first + (i + 1) * chunk // 2)
                    normed[at, :] = got[: chunk // 2]
                    other[at, :] = got[chunk // 2 :]
            else:
                at = slice(first, first + size)
                if lengths[p] == 1:
                    normed[at, :] = sources[p][0][:size, :]
                    other[at, :] = sources[p][0][size:, :]
                else:
                    head, rest = sources[p]
                    early = head.shape[0]
                    late = size - early
                    normed[at, :] = rest[late:, :]
                    other[first : first + early, :] = head[...]
                    other[first + early : first + size, :] = rest[:late, :]

    def wait(i, j):
        @pl.when(step == 0)
        def _():
            for copy in copies[i:j]:
                copy.wait()

    wait(4, 6)
    back[...] = lax.dot_general(
        other[...], weights[2 * half :, :], TRANS, preferred_element_type=F32
    )
    wait(0, 4)
    both[...] = lax.dot_general(
        normed[...], weights[: 2 * half, :], TRANS, preferred_element_type=F32
    )
    gate, up, dy = both[:, :half], both[:, half:], back[...]
    sig = jax.nn.sigmoid(gate)
    active = gate * sig
    grad_up = dy * active
    grads[:, half:] = grad_up.astype(BF)
    grads[:, :half] = (dy * up * (sig + active * (1.0 - sig))).astype(BF)
    score = jnp.sum(grad_up * up, -1, keepdims=True)
    joint[...] = jnp.broadcast_to(score, joint.shape)
    if mixed:
        other[...] = jnp.dot(
            grads[...], weights[: 2 * half, :], preferred_element_type=F32
        ).astype(BF)
        chunk = table.shape[0]
        for i in range(2 * normed.shape[0] // chunk):
            at = slice(i * chunk // 2, (i + 1) * chunk // 2)
            sides = jnp.concatenate([other[at, : width // 2], other[at, width // 2 :]], 0)
            into[i * chunk : (i + 1) * chunk, :] = jnp.dot(
                table_back[...], sides, preferred_element_type=F32
            ).astype(BF)
    else:
        into[...] = jnp.dot(
            grads[...], weights[: 2 * half, :], preferred_element_type=F32
        ).astype(BF)


def hidden_grads(sources, pieces, tables=()):
    count = len(sources)
    lengths = [len(v) for v in sources]
    mixed = len(tables) > 0
    size = sources[0][0].shape[0] // 2
    sources = [v for source in sources for v in source]
    part, width = pieces[0].shape
    half = -(-2 * part // 128) * 128
    total = count * size
    step_rows = min(total, 320) if mixed else 2 * size
    out = (2 * total, width // 2) if mixed else (total, width)
    block = (2 * step_rows, width // 2) if mixed else (step_rows, width)

    def whole(value):
        return pl.BlockSpec(value.shape, lambda i: (0, 0), pipeline_mode=pl.Buffered(1))

    into, joint = pl.pallas_call(
        lambda *refs: hidden_kernel(lengths, mixed, *refs),
        grid=(total // step_rows,),
        in_specs=[whole(v) for v in sources]
        + [pl.BlockSpec(memory_space=pl.ANY)] * 6
        + [whole(v) for v in tables],
        out_specs=[
            pl.BlockSpec(block, lambda i: (i, 0)),
            pl.BlockSpec((step_rows, 128), lambda i: (i, 0)),
        ],
        out_shape=[jax.ShapeDtypeStruct(out, BF), jax.ShapeDtypeStruct((total, 128), F32)],
        scratch_shapes=[
            pltpu.VMEM((3 * half, width), BF),
            pltpu.VMEM((step_rows, width), BF),
            pltpu.VMEM((step_rows, width), BF),
            pltpu.VMEM((step_rows, 2 * half), F32),
            pltpu.VMEM((step_rows, half), F32),
            pltpu.VMEM((step_rows, 2 * half), BF),
            pltpu.SemaphoreType.DMA((6,)),
        ],
        compiler_params=pltpu.CompilerParams(vmem_limit_bytes=VMEM_LIMIT),
        cost_estimate=pl.CostEstimate(
            flops=10 * total * width * half,
            bytes_accessed=6 * half * width + 6 * total * width,
            transcendentals=total * half,
        ),
    )(*sources, *pieces, *tables)
    return into, joint[:, 0]


def pick_kernel(table, rows, out):
    out[...] = jnp.dot(table[...], rows[...], preferred_element_type=F32).astype(BF)


def pick_rows(table, source):
    rows, depth = table.shape
    width = source.shape[1]
    block = 512 if width % 512 == 0 else 128
    return pl.pallas_call(
        pick_kernel,
        grid=(width // block,),
        in_specs=[
            pl.BlockSpec((rows, depth), lambda i: (0, 0)),
            pl.BlockSpec((depth, block), lambda i: (0, i)),
        ],
        out_specs=pl.BlockSpec((rows, block), lambda i: (0, i)),
        out_shape=jax.ShapeDtypeStruct((rows, width), BF),
        compiler_params=pltpu.CompilerParams(vmem_limit_bytes=VMEM_LIMIT),
        cost_estimate=pl.CostEstimate(
            flops=2 * rows * depth * width,
            bytes_accessed=2 * width * (rows + depth),
            transcendentals=0,
        ),
    )(table, source)


def slots_of(routes, experts):
    tok = routes.shape[0]
    flat = routes.reshape(2 * tok, 1)
    hits = (flat == lax.broadcasted_iota(jnp.int32, (1, experts), 1)).astype(BF)
    place = lax.broadcasted_iota(jnp.int32, (2 * tok, 2 * tok), 0)
    before = (lax.broadcasted_iota(jnp.int32, (2 * tok, 2 * tok), 1) < place).astype(BF)
    places = jnp.dot(before, hits, preferred_element_type=F32)
    return jnp.sum(hits.astype(F32) * places, -1).astype(jnp.int32).reshape(tok, 2)


def spread(index, rows):
    return index[..., None] == lax.broadcasted_iota(jnp.int32, (1, 1, rows), 2)


def picker(index, rows):
    hits = lax.broadcasted_iota(jnp.int32, (rows, 1), 0)
    return (hits == index[:, 0][None]).astype(BF) + (hits == index[:, 1][None]).astype(BF)


def router_weights(normed, router, chosen):
    logits = jnp.dot(normed.astype(F32), router, precision=HIGHEST)
    picked = jnp.sum(jnp.where(chosen, logits[:, None, :], 0.0), -1)
    one = jax.nn.sigmoid(picked[:, 0:1] - picked[:, 1:2])
    return jnp.concatenate([one, 1.0 - one], 1)


def mix(index, weights, rows, cap):
    count = rows.shape[0]
    tables = []
    for shift in (0, cap):
        hot = spread(index + shift, count)
        tables.append(jnp.sum(jnp.where(hot, weights[..., None], 0.0), 1).astype(BF))
    tok = index.shape[0]
    sides = jnp.dot(jnp.concatenate(tables, 0), rows, preferred_element_type=F32)
    return jnp.concatenate([sides[:tok], sides[tok:]], 1)


def body(
    tokens,
    cotangent,
    norm_gain,
    router,
    dense_gate,
    dense_up,
    dense_down,
    expert_gate,
    expert_up,
    expert_down,
    routes,
):
    tok, width = tokens.shape
    experts = router.shape[1]
    cap = 5 * tok // (2 * experts)
    block = 2 * cap
    everything = experts * block

    values = tokens.astype(F32)
    inverse = lax.rsqrt(jnp.mean(values * values, -1, keepdims=True) + EPS)
    normed = (values * inverse * norm_gain).astype(BF)
    pair = jnp.concatenate([normed, cotangent], 0)

    early = tok // 2
    peer_cot = {k: receive_from(cotangent[:early], k) for k in (1, 3)}
    expert = weight_pieces(expert_gate[0], expert_up[0], expert_down[0])
    far_routes = receive_from(routes, 2)

    def pick_for(rows, index):
        places = jnp.concatenate([index, index + cap], 0)
        return pick_rows(picker(places, everything), rows)

    own_index = routes * block + slots_of(routes, experts)
    far_index = far_routes * block + slots_of(far_routes, experts)
    ready = tuple(peer_cot.values()) + (expert[1], expert[3], far_routes)
    own_send = after(pick_for(pair, own_index), *ready)
    own = over(own_send)
    far_pair = receive_from(pair, 2)
    others = jnp.concatenate([cotangent[early:], normed], 0)
    peer_rest = {k: receive_from(others, k) for k in (1, 3)}
    dense = weight_pieces(*(after(v, own_send) for v in (dense_gate, dense_up, dense_down)))
    chunk = everything // 2
    parts = [own[:chunk], own[chunk:]]
    near = [{k: receive_from(part, k) for k in (1, 3)} for part in parts]
    far = over(pick_for(after(far_pair, *parts), far_index))
    table = shuffle_table(cap, experts // 2)
    tables = (table, table.T)

    own_into, own_joint = hidden_grads([(own,)], expert, tables)
    dense_part, unused = hidden_grads(
        [
            (after(pair, own_into),),
            (peer_cot[1], peer_rest[1]),
            (far_pair,),
            (peer_cot[3], peer_rest[3]),
        ],
        dense,
    )
    far_into, far_joint = hidden_grads([(after(far, dense_part),)], expert, tables)
    far_back = over(far_into)
    near_into = [None, None]
    near_joint = [None, None]
    near_into[0], near_joint[0] = hidden_grads(
        [(after(near[0][1], far_into),), (near[0][3],)], expert, tables
    )
    near_into[1], near_joint[1] = hidden_grads(
        [(after(near[1][1], near_into[0]),), (near[1][3],)], expert, tables
    )
    near_into[1] = after(near_into[1], far_back)
    arrived = (near[1][1], near[1][3])
    home1 = send_to(after(dense_part[tok : 2 * tok], *arrived), 1)
    home3 = send_to(after(dense_part[3 * tok :], *arrived), 3)
    near_back = []
    for i in (0, 1):
        first = after(near_into[i], home1, home3) if i == 0 else near_into[i]
        near_back.append(send_to(first[:chunk], 1).astype(F32) + send_to(first[chunk:], 3).astype(F32))

    joints = jnp.stack(
        [
            own_joint.reshape(experts, cap),
            jnp.concatenate([v[: chunk // 2] for v in near_joint]).reshape(experts, cap),
            far_joint.reshape(experts, cap),
            jnp.concatenate([v[chunk // 2 :] for v in near_joint]).reshape(experts, cap),
        ],
        1,
    )
    joints = over(after(joints.reshape(experts, PEERS * cap), far_back))
    joints = joints.reshape(experts, PEERS, cap)
    shares = [send_to(joints[:, k], k) for k in (1, 2, 3)]

    own_sum = own_into.astype(F32) + jnp.concatenate(near_back, 0)
    own_sum = after(own_sum.astype(BF), joints)
    own_back = over(own_sum)
    score = after(joints[:, 0], own_sum)
    for share in shares:
        score = score + share

    ids = lax.broadcasted_iota(jnp.int32, (1, 1, experts), 2)
    chosen = routes[..., None] == ids
    weights = router_weights(normed, router, chosen)
    far_weights = router_weights(far_pair[:tok], router, far_routes[..., None] == ids)
    mixed = dense_part[2 * tok : 3 * tok].astype(F32)
    mixed = mixed + mix(far_index, far_weights, far_back, cap)
    home2 = send_to(mixed.astype(BF), 2)

    scores = jnp.sum(
        jnp.where(
            spread(routes * cap + own_index - routes * block, experts * cap),
            score.reshape(1, 1, -1),
            0.0,
        ),
        -1,
    )
    delta = weights[:, 0] * weights[:, 1] * (scores[:, 0] - scores[:, 1])
    signed = chosen[:, 0].astype(F32) - chosen[:, 1].astype(F32)
    grad_logits = signed * delta[:, None]
    local_router = lax.dot_general(
        grad_logits, normed.astype(F32), (((0,), (0,)), ((), ())), precision=HIGHEST
    )
    known = dense_part[:tok].astype(F32)
    known = known + jnp.dot(grad_logits, router.T, precision=HIGHEST)
    for piece in (home1, home3):
        known = known + piece.astype(F32)

    total = known + home2.astype(F32) + mix(own_index, weights, own_back, cap)
    local_gain = jnp.sum(total * values * inverse, 0, keepdims=True)
    axes = ("ep", "y", "core")
    devices = lax.axis_size(axes)
    local = jnp.concatenate([local_router, local_gain], 0).reshape(devices, -1)
    mine = jnp.sum(over(local, axes), 0, keepdims=True)
    sums = over(jnp.broadcast_to(mine, local.shape), axes).reshape(experts + 1, width)
    scaled = total * norm_gain
    mean_term = jnp.mean(scaled * values, -1, keepdims=True)
    input_grad = cotangent.astype(F32) + inverse * (
        scaled - values * inverse * inverse * mean_term
    )
    return (input_grad.astype(BF), sums[experts], sums[:experts].T)


def solution(mesh):
    ep, sp = mesh.devices.shape
    grid = Mesh(mesh.devices.reshape(ep, sp // 2, 2), ("ep", "y", "core"))
    shared = ("y", "core")
    rows = ("ep", "y", "core")
    return jax.shard_map(
        body,
        mesh=grid,
        in_specs=(
            P(rows, None),
            P(rows, None),
            P(),
            P(),
            P(None, shared),
            P(None, shared),
            P(shared, None),
            P("ep", None, shared),
            P("ep", None, shared),
            P("ep", shared, None),
            P(rows, None),
        ),
        out_specs=(P(rows, None), P(), P()),
        check_vma=False,
    )
```

profile of v0, /device:TPU:1, one launch (start us, length us, event | category | flops | bytes accessed | tf_op | source)
XLA Modules:
  0.0 391.6 jit_solution(11475134969568275216)
XLA Ops:
  0.7 2.1 fusion.84
  2.8 3.6 collective-permute-start
  7.3 1.9 collective-permute-start.4
  14.1 4.9 %shard_map.130 = bf16[640,3584]{1,0:T(8,128)(2,1)} custom-call(bf16[640,256]{1,0:T(8,128)(2,1)S(1)} %fusion.47.table, bf16[256,3584]{1,0:T(8,128)(2,1)S(1)} %pad_maximum_fusion.rows.refs_0_), custom_call_target="tpu_custom_call" | custom-call | flops 1174405120 | bytes 6422528 | tf_op jit(solution)/shard_map/pallas_call | solution.py:206
  19.9 7.7 %all-to-all-start = ((bf16[16,40,3584]{2,1,0:T(8,128)(2,1)}), bf16[16,40,3584]{2,1,0:T(8,128)(2,1)}, u32[]{:S(2)}, u32[]{:S(2)}) async-start(bf16[16,40,3584]{2,1,0:T(8,128)(2,1)} %bitcast.57), calls=%async_computation | async-start | bytes 9175040 | tf_op jit(solution)/shard_map/all_to_all | solution.py:30
  28.8 2.4 pad_maximum_fusion.1
  31.2 3.0 collective-permute-start.6
  38.1 45.7 %all-to-all-done = bf16[16,40,3584]{2,1,0:T(8,128)(2,1)} async-done(((bf16[16,40,3584]{2,1,0:T(8,128)(2,1)}), bf16[16,40,3584]{2,1,0:T(8,128)(2,1)}, u32[]{:S(2)}, u32[]{:S(2)}) %all-to-all-start) | async-done | bytes 4587552 | tf_op jit(solution)/shard_map/all_to_all | solution.py:30
  83.7 4.8 %fusion.78 = (bf16[8,40,3584]{2,1,0:T(8,128)(2,1)}, bf16[8,40,3584]{2,1,0:T(8,128)(2,1)}) fusion(bf16[16,40,3584]{2,1,0:T(8,128)(2,1)} %all-to-all-done), kind=kLoop, calls=%fused_computation.156 | loop fusion | bytes 9175040 | tf_op jit(solution)/shard_map/slice | solution.py:304
  88.5 6.7 %shard_map.133 = bf16[640,3584]{1,0:T(8,128)(2,1)} custom-call(bf16[640,256]{1,0:T(8,128)(2,1)S(1)} %fusion.46.table, bf16[256,3584]{1,0:T(8,128)(2,1)} %collective-permute-done.7.refs_3_.rows), custom_call_target="tpu_custom_call" | custom-call | flops 1174405120 | bytes 6422528 | tf_op jit(solution)/shard_map/pallas_call | solution.py:206
  95.3 11.2 %all-to-all-start.1 = ((bf16[16,40,3584]{2,1,0:T(8,128)(2,1)}), bf16[16,40,3584]{2,1,0:T(8,128)(2,1)}, u32[]{:S(2)}, u32[]{:S(2)}) async-start(bf16[16,40,3584]{2,1,0:T(8,128)(2,1)} %bitcast.56), calls=%async_computation.1 | async-start | bytes 9175040 | tf_op jit(solution)/shard_map/all_to_all | solution.py:30
  106.4 3.7 collective-permute-start.10
  111.8 2.0 fusion.24
  114.1 11.9 %collective-permute-start.14 = (bf16[320,3584]{1,0:T(8,128)(2,1)}, bf16[320,3584]{1,0:T(8,128)(2,1)}, u32[]{:S(2)}, u32[]{:S(2)}) collective-permute-start(bf16[320,3584]{1,0:T(8,128)(2,1)} %bitcast.61), channel_id=1, source_target_pairs={{0,6},{2,0},{4,2},{6,4},{1,7},{3,1},{5,3},{7,5},{8,14},{10,8},{12,... | collective-permute-start | bytes 6881288 | tf_op jit(solution)/shard_map/ppermute | solution.py:18
  126.2 17.4 %shard_map.131 = (bf16[640,1792]{1,0:T(8,128)(2,1)}, f32[320,128]{1,0:T(8,128)S(1)}) custom-call(bf16[640,3584]{1,0:T(8,128)(2,1)} %bitcast.7.refs_0_, bf16[304,3584]{1,0:T(8,128)(2,1)S(1)} %bitcast.52, bf16[304,3584]{1,0:T(8,128)(2,1)} %collective-permute-done.2.refs_2_.refs_3_, bf16[304,3584]{1,0:T(8,128)(2,1)} %bitcast.77, ...), custom_call_target="tpu_custom_call" | custom-call | flops 7340032000 | bytes 20643840 | tf_op jit(solution)/shard_map/pallas_call | solution.py:168
  144.5 2.6 collective-permute-start.12
  149.4 22.2 %shard_map.132 = (bf16[512,3584]{1,0:T(8,128)(2,1)}, f32[512,128]{1,0:T(8,128)}) custom-call(bf16[256,3584]{1,0:T(8,128)(2,1)} %copy-done.1, bf16[64,3584]{1,0:T(8,128)(2,1)S(1)} %copy-done.4, bf16[192,3584]{1,0:T(8,128)(2,1)} %collective-permute-done.6.refs_2_, bf16[256,3584]{1,0:T(8,128)(2,1)} %collective-permute-done.7.refs_3_.rows, ...), custom_call_target="tpu_custom_call" | custom-call | flops 11744051200 | bytes 24772608 | tf_op jit(solution)/shard_map/pallas_call | solution.py:168
  171.6 2.8 fusion.79
  174.4 1.9 collective-permute-done.14.refs_0_
  176.3 2.5 collective-permute-done.15.refs_1_
  180.6 17.3 %shard_map.134 = (bf16[640,1792]{1,0:T(8,128)(2,1)}, f32[320,128]{1,0:T(8,128)S(1)}) custom-call(bf16[640,3584]{1,0:T(8,128)(2,1)} %bitcast.17.refs_0_, bf16[304,3584]{1,0:T(8,128)(2,1)S(1)} %bitcast.53, bf16[304,3584]{1,0:T(8,128)(2,1)} %collective-permute-done.2.refs_2_.refs_3_, bf16[304,3584]{1,0:T(8,128)(2,1)} %bitcast.78, ...), custom_call_target="tpu_custom_call" | custom-call | flops 7340032000 | bytes 20643840 | tf_op jit(solution)/shard_map/pallas_call | solution.py:168
  197.9 7.1 %all-to-all-start.2 = ((bf16[16,40,1792]{2,1,0:T(8,128)(2,1)}), bf16[16,40,1792]{2,1,0:T(8,128)(2,1)}, u32[]{:S(2)}, u32[]{:S(2)}) async-start(bf16[16,40,1792]{2,1,0:T(8,128)(2,1)} %bitcast.63), calls=%async_computation.2 | async-start | bytes 4587520 | tf_op jit(solution)/shard_map/all_to_all | solution.py:30
  205.1 20.4 %collective-permute-done.12.refs_0_ = bf16[320,3584]{1,0:T(8,128)(2,1)} collective-permute-done((bf16[320,3584]{1,0:T(8,128)(2,1)}, bf16[320,3584]{1,0:T(8,128)(2,1)}, u32[]{:S(2)}, u32[]{:S(2)}) %collective-permute-start.12) | collective-permute-done | bytes 2293792 | tf_op jit(solution)/shard_map/ppermute | solution.py:18
  225.4 2.5 collective-permute-done.13.refs_1_
  227.9 17.5 %shard_map.135 = (bf16[640,1792]{1,0:T(8,128)(2,1)}, f32[320,128]{1,0:T(8,128)S(1)}) custom-call(bf16[320,3584]{1,0:T(8,128)(2,1)} %collective-permute-done.12.refs_0_, bf16[320,3584]{1,0:T(8,128)(2,1)} %collective-permute-done.13.refs_1_, bf16[304,3584]{1,0:T(8,128)(2,1)S(1)} %bitcast.54, bf16[304,3584]{1,0:T(8,128)(2,1)} %collective-permute-done.2.refs_2_.refs_3_, ...), custom_call_target="tpu_custom_call" | custom-call | flops 7340032000 | bytes 20643840 | tf_op jit(solution)/shard_map/pallas_call | solution.py:168
  245.4 2.2 collective-permute-done.16
  247.6 3.1 fusion.80
  250.7 2.9 collective-permute-start.19
  253.6 17.5 %shard_map.136 = (bf16[640,1792]{1,0:T(8,128)(2,1)}, f32[320,128]{1,0:T(8,128)S(1)}) custom-call(bf16[320,3584]{1,0:T(8,128)(2,1)} %collective-permute-done.14.refs_0_, bf16[320,3584]{1,0:T(8,128)(2,1)} %collective-permute-done.15.refs_1_, bf16[304,3584]{1,0:T(8,128)(2,1)S(1)} %bitcast.55, bf16[304,3584]{1,0:T(8,128)(2,1)} %collective-permute-done.2.refs_2_.refs_3_, ...), custom_call_target="tpu_custom_call" | custom-call | flops 7340032000 | bytes 20643840 | tf_op jit(solution)/shard_map/pallas_call | solution.py:168
  273.3 3.2 fusion.81
  276.5 2.7 collective-permute-start.21
  279.2 1.8 convert_add_fusion.1
  281.0 7.1 %all-to-all-start.3 = ((f32[16,1,80]{2,1,0:T(1,128)}), f32[16,1,80]{2,1,0:T(1,128)S(1)}, u32[]{:S(2)}, u32[]{:S(2)}) async-start(f32[16,1,80]{2,1,0:T(1,128)} %bitcast.23), calls=%async_computation.3 | async-start | bytes 16384 | tf_op jit(solution)/shard_map/all_to_all | solution.py:30
  288.2 2.5 fusion.48
  292.0 2.4 all-to-all-done.3
  295.9 2.4 collective-permute-start.23
  298.5 4.6 %collective-permute-done.20 = bf16[320,1792]{1,0:T(8,128)(2,1)} collective-permute-done((bf16[320,1792]{1,0:T(8,128)(2,1)}, bf16[320,1792]{1,0:T(8,128)(2,1)}, u32[]{:S(2)}, u32[]{:S(2)}) %collective-permute-start.20) | collective-permute-done | bytes 1146912 | tf_op jit(solution)/shard_map/ppermute | solution.py:22
  305.0 2.0 fusion
  307.0 6.9 %all-to-all-start.4 = ((bf16[16,40,1792]{2,1,0:T(8,128)(2,1)}), bf16[16,40,1792]{2,1,0:T(8,128)(2,1)S(1)}, u32[]{:S(2)}, u32[]{:S(2)}) async-start(bf16[16,40,1792]{2,1,0:T(8,128)(2,1)} %bitcast.29), calls=%async_computation.4 | async-start | bytes 4587520 | tf_op jit(solution)/shard_map/all_to_all | solution.py:30
  313.9 2.9 fusion.13
  319.4 2.9 fusion.60
  322.5 18.5 %all-to-all-done.4 = bf16[16,40,1792]{2,1,0:T(8,128)(2,1)S(1)} async-done(((bf16[16,40,1792]{2,1,0:T(8,128)(2,1)}), bf16[16,40,1792]{2,1,0:T(8,128)(2,1)S(1)}, u32[]{:S(2)}, u32[]{:S(2)}) %all-to-all-start.4) | async-done | bytes 2293792 | tf_op jit(solution)/shard_map/all_to_all | solution.py:30
  343.7 4.3 %fusion.12 = (f32[3584]{0:T(1024)S(1)}, f32[128]{0:T(128)S(1)}, f32[128,3584]{1,0:T(8,128)}) fusion(bf16[128,3584]{1,0:T(8,128)(2,1)S(1)} %copy-done.11, f32[128]{0:T(128)S(1)} %copy-done.25, f32[3584]{0:T(1024)S(1)} %copy-done.17, f32[128,1792]{1,0:T(8,128)S(1)} %get-tuple-element.83, f32[128,1792]{1,0:T(8,128)S(1)} %get-tuple-element.82, ...), kind=kLoop, calls=%fused_computation.19 | loop fusion | flops 7795072 | bytes 10122240 | tf_op jit(solution)/shard_map/reduce_sum | solution.py:387
  349.2 12.2 %all-to-all-start.5 = ((f32[128,1,476]{2,1,0:T(1,128)}), f32[128,1,476]{2,1,0:T(1,128)S(1)}, u32[]{:S(2)}, u32[]{:S(2)}) async-start(f32[128,1,476]{2,1,0:T(1,128)} %all_to_all.64), calls=%async_computation.5 | async-start | bytes 524288 | tf_op jit(solution)/shard_map/all_to_all | solution.py:30
  361.5 10.8 %all-to-all-done.5 = f32[128,1,476]{2,1,0:T(1,128)S(1)} async-done(((f32[128,1,476]{2,1,0:T(1,128)}), f32[128,1,476]{2,1,0:T(1,128)S(1)}, u32[]{:S(2)}, u32[]{:S(2)}) %all-to-all-start.5) | async-done | bytes 243744 | tf_op jit(solution)/shard_map/all_to_all | solution.py:30
  373.3 4.8 %all-to-all-start.6 = ((f32[128,1,476]{2,1,0:T(1,128)}), f32[128,1,476]{2,1,0:T(1,128)S(1)}, u32[]{:S(2)}, u32[]{:S(2)}) async-start(f32[128,1,476]{2,1,0:T(1,128)} %broadcast_in_dim.95), calls=%async_computation.6 | async-start | bytes 524288 | tf_op jit(solution)/shard_map/all_to_all | solution.py:30
  378.1 3.1 fusion.8
  381.1 7.7 %all-to-all-done.6 = f32[128,1,476]{2,1,0:T(1,128)S(1)} async-done(((f32[128,1,476]{2,1,0:T(1,128)}), f32[128,1,476]{2,1,0:T(1,128)S(1)}, u32[]{:S(2)}, u32[]{:S(2)}) %all-to-all-start.6) | async-done | bytes 243744 | tf_op jit(solution)/shard_map/all_to_all | solution.py:30
  (168 shorter events, 35.8 us)
Async XLA Ops:
  0.6 35.1 %copy-start = (f32[3584,16]{0,1:T(8,128)S(1)}, f32[3584,16]{0,1:T(8,128)}, u32[]{:S(2)}) copy-start(f32[3584,16]{0,1:T(8,128)} %param.14) | copy-start | bytes 688132
  0.6 6.7 %copy-start.18 = (s32[128,2]{0,1:T(2,128)S(1)}, s32[128,2]{0,1:T(2,128)}, u32[]{:S(2)}) copy-start(s32[128,2]{0,1:T(2,128)} %param.21) | copy-start | bytes 3076
  0.7 9.8 %copy-start.10 = (bf16[128,3584]{1,0:T(8,128)(2,1)S(1)}, bf16[128,3584]{1,0:T(8,128)(2,1)}, u32[]{:S(2)}) copy-start(bf16[128,3584]{1,0:T(8,128)(2,1)} %param.11) | copy-start | bytes 2752516
  0.7 10.7 %copy-start.16 = (f32[3584]{0:T(1024)S(1)}, f32[3584]{0:T(1024)}, u32[]{:S(2)}) copy-start(f32[3584]{0:T(1024)} %param.13) | copy-start | bytes 43012
  2.8 16.2 %collective-permute-start = (bf16[64,3584]{1,0:T(8,128)(2,1)}, bf16[64,3584]{1,0:T(8,128)(2,1)S(1)}, u32[]{:S(2)}, u32[]{:S(2)}) collective-permute-start(bf16[64,3584]{1,0:T(8,128)(2,1)} %get-tuple-element.85), channel_id=1, source_target_pairs={{0,6},{2,0},{4,2},{6,4},{1,7},{3,1},{5,3},{7,5},{8,14},{10,8},{12,... | collective-permute-start | bytes 1376264 | tf_op jit(solution)/shard_map/ppermute | solution.py:18
  6.4 12.7 %collective-permute-start.1 = (bf16[64,3584]{1,0:T(8,128)(2,1)}, bf16[64,3584]{1,0:T(8,128)(2,1)S(1)}, u32[]{:S(2)}, u32[]{:S(2)}) collective-permute-start(bf16[64,3584]{1,0:T(8,128)(2,1)} %get-tuple-element.85), channel_id=1, source_target_pairs={{0,2},{2,4},{4,6},{6,0},{1,3},{3,5},{5,7},{7,1},{8,10},{10,12},{12... | collective-permute-start | bytes 1376264 | tf_op jit(solution)/shard_map/ppermute | solution.py:18
  6.4 12.7 %collective-permute-start.2 = (bf16[304,3584]{1,0:T(8,128)(2,1)}, bf16[304,3584]{1,0:T(8,128)(2,1)}, u32[]{:S(2)}, u32[]{:S(2)}) collective-permute-start(bf16[304,3584]{1,0:T(8,128)(2,1)} %bitcast.51), channel_id=1, source_target_pairs={{0,1},{1,0},{2,3},{3,2},{4,5},{5,4},{6,7},{7,6},{8,9},{9,8},{10,11... | collective-permute-start | bytes 6537224 | tf_op jit(solution)/shard_map/ppermute | solution.py:26
  7.3 11.7 %collective-permute-start.3 = (bf16[304,3584]{1,0:T(8,128)(2,1)}, bf16[304,3584]{1,0:T(8,128)(2,1)}, u32[]{:S(2)}, u32[]{:S(2)}) collective-permute-start(bf16[304,3584]{1,0:T(8,128)(2,1)} %bitcast.76), channel_id=1, source_target_pairs={{0,1},{1,0},{2,3},{3,2},{4,5},{5,4},{6,7},{7,6},{8,9},{9,8},{10,11... | collective-permute-start | bytes 6537224 | tf_op jit(solution)/shard_map/ppermute | solution.py:26
  7.3 11.7 %collective-permute-start.4 = (s32[128,2]{0,1:T(2,128)S(1)}, s32[128,2]{0,1:T(2,128)S(1)}, u32[]{:S(2)}, u32[]{:S(2)}) collective-permute-start(s32[128,2]{0,1:T(2,128)S(1)} %copy-done.18), channel_id=1, source_target_pairs={{0,4},{2,6},{4,0},{6,2},{1,5},{3,7},{5,1},{7,3},{8,12},{10,14},{12... | collective-permute-start | bytes 3080 | tf_op jit(solution)/shard_map/ppermute | solution.py:18
  13.3 14.4 %copy-start.1 = (bf16[256,3584]{1,0:T(8,128)(2,1)}, bf16[256,3584]{1,0:T(8,128)(2,1)S(1)}, u32[]{:S(2)}) copy-start(bf16[256,3584]{1,0:T(8,128)(2,1)S(1)} %pad_maximum_fusion.rows.refs_0_) | copy-start | bytes 5505028
  19.9 63.8 %all-to-all-start = ((bf16[16,40,3584]{2,1,0:T(8,128)(2,1)}), bf16[16,40,3584]{2,1,0:T(8,128)(2,1)}, u32[]{:S(2)}, u32[]{:S(2)}) async-start(bf16[16,40,3584]{2,1,0:T(8,128)(2,1)} %bitcast.57), calls=%async_computation | async-start | bytes 9175040 | tf_op jit(solution)/shard_map/all_to_all | solution.py:30
  27.6 8.1 %copy-start.8 = (bf16[128,3584]{1,0:T(8,128)(2,1)S(1)}, bf16[128,3584]{1,0:T(8,128)(2,1)}, u32[]{:S(2)}) copy-start(bf16[128,3584]{1,0:T(8,128)(2,1)} %copy-done.7) | copy-start | bytes 2752516
  27.6 60.9 %collective-permute-start.7 = (bf16[256,3584]{1,0:T(8,128)(2,1)S(1)}, bf16[256,3584]{1,0:T(8,128)(2,1)}, u32[]{:S(2)}, u32[]{:S(2)}) collective-permute-start(bf16[256,3584]{1,0:T(8,128)(2,1)S(1)} %pad_maximum_fusion.rows.refs_0_), channel_id=1, source_target_pairs={{0,4},{2,6},{4,0},{6,2},{1,5},{3,7},{5,1},{7,3},{8,12},{10,14},{12... | collective-permute-start | bytes 5505032 | tf_op jit(solution)/shard_map/ppermute | solution.py:18
  31.2 79.1 %collective-permute-start.6 = (bf16[192,3584]{1,0:T(8,128)(2,1)}, bf16[192,3584]{1,0:T(8,128)(2,1)}, u32[]{:S(2)}, u32[]{:S(2)}) collective-permute-start(bf16[192,3584]{1,0:T(8,128)(2,1)} %pad_maximum_fusion.1), channel_id=1, source_target_pairs={{0,6},{2,0},{4,2},{6,4},{1,7},{3,1},{5,3},{7,5},{8,14},{10,8},{12,... | collective-permute-start | bytes 4128776 | tf_op jit(solution)/shard_map/ppermute | solution.py:18
  34.2 80.0 %collective-permute-start.8 = (bf16[192,3584]{1,0:T(8,128)(2,1)}, bf16[192,3584]{1,0:T(8,128)(2,1)}, u32[]{:S(2)}, u32[]{:S(2)}) collective-permute-start(bf16[192,3584]{1,0:T(8,128)(2,1)} %pad_maximum_fusion.1), channel_id=1, source_target_pairs={{0,2},{2,4},{4,6},{6,0},{1,3},{3,5},{5,7},{7,1},{8,10},{10,12},{12... | collective-permute-start | bytes 4128776 | tf_op jit(solution)/shard_map/ppermute | solution.py:18
  34.2 91.8 %collective-permute-start.5 = (bf16[304,3584]{1,0:T(8,128)(2,1)}, bf16[304,3584]{1,0:T(8,128)(2,1)}, u32[]{:S(2)}, u32[]{:S(2)}) collective-permute-start(bf16[304,3584]{1,0:T(8,128)(2,1)} %bitcast.81), channel_id=1, source_target_pairs={{0,1},{1,0},{2,3},{3,2},{4,5},{5,4},{6,7},{7,6},{8,9},{9,8},{10,11... | collective-permute-start | bytes 6537224 | tf_op jit(solution)/shard_map/ppermute | solution.py:26
  95.2 30.9 %copy-start.2 = (bf16[1,3584,304]{1,2,0:T(8,128)(2,1)S(1)}, bf16[1,3584,304]{1,2,0:T(8,128)(2,1)}, u32[]{:S(2)}) copy-start(bf16[1,3584,304]{1,2,0:T(8,128)(2,1)} %param.18) | copy-start | bytes 6537220
  95.3 85.4 %all-to-all-start.1 = ((bf16[16,40,3584]{2,1,0:T(8,128)(2,1)}), bf16[16,40,3584]{2,1,0:T(8,128)(2,1)}, u32[]{:S(2)}, u32[]{:S(2)}) async-start(bf16[16,40,3584]{2,1,0:T(8,128)(2,1)} %bitcast.56), calls=%async_computation.1 | async-start | bytes 9175040 | tf_op jit(solution)/shard_map/all_to_all | solution.py:30
  106.4 38.0 %collective-permute-start.10 = (bf16[304,3584]{1,0:T(8,128)(2,1)}, bf16[304,3584]{1,0:T(8,128)(2,1)}, u32[]{:S(2)}, u32[]{:S(2)}) collective-permute-start(bf16[304,3584]{1,0:T(8,128)(2,1)} %bitcast.74), channel_id=1, source_target_pairs={{0,1},{1,0},{2,3},{3,2},{4,5},{5,4},{6,7},{7,6},{8,9},{9,8},{10,11... | collective-permute-start | bytes 6537224 | tf_op jit(solution)/shard_map/ppermute | solution.py:26
  110.2 37.0 %collective-permute-start.11 = (bf16[304,3584]{1,0:T(8,128)(2,1)}, bf16[304,3584]{1,0:T(8,128)(2,1)}, u32[]{:S(2)}, u32[]{:S(2)}) collective-permute-start(bf16[304,3584]{1,0:T(8,128)(2,1)} %refs_10_), channel_id=1, source_target_pairs={{0,1},{1,0},{2,3},{3,2},{4,5},{5,4},{6,7},{7,6},{8,9},{9,8},{10,11... | collective-permute-start | bytes 6537224 | tf_op jit(solution)/shard_map/ppermute | solution.py:26
  110.3 37.1 %collective-permute-start.9 = (bf16[304,3584]{1,0:T(8,128)(2,1)}, bf16[304,3584]{1,0:T(8,128)(2,1)}, u32[]{:S(2)}, u32[]{:S(2)}) collective-permute-start(bf16[304,3584]{1,0:T(8,128)(2,1)} %bitcast.72), channel_id=1, source_target_pairs={{0,1},{1,0},{2,3},{3,2},{4,5},{5,4},{6,7},{7,6},{8,9},{9,8},{10,11... | collective-permute-start | bytes 6537224 | tf_op jit(solution)/shard_map/ppermute | solution.py:26
  114.1 62.1 %collective-permute-start.14 = (bf16[320,3584]{1,0:T(8,128)(2,1)}, bf16[320,3584]{1,0:T(8,128)(2,1)}, u32[]{:S(2)}, u32[]{:S(2)}) collective-permute-start(bf16[320,3584]{1,0:T(8,128)(2,1)} %bitcast.61), channel_id=1, source_target_pairs={{0,6},{2,0},{4,2},{6,4},{1,7},{3,1},{5,3},{7,5},{8,14},{10,8},{12,... | collective-permute-start | bytes 6881288 | tf_op jit(solution)/shard_map/ppermute | solution.py:18
  126.0 52.7 %collective-permute-start.15 = (bf16[320,3584]{1,0:T(8,128)(2,1)}, bf16[320,3584]{1,0:T(8,128)(2,1)}, u32[]{:S(2)}, u32[]{:S(2)}) collective-permute-start(bf16[320,3584]{1,0:T(8,128)(2,1)} %bitcast.62), channel_id=1, source_target_pairs={{0,2},{2,4},{4,6},{6,0},{1,3},{3,5},{5,7},{7,1},{8,10},{10,12},{12... | collective-permute-start | bytes 6881288 | tf_op jit(solution)/shard_map/ppermute | solution.py:18
  144.5 80.9 %collective-permute-start.12 = (bf16[320,3584]{1,0:T(8,128)(2,1)}, bf16[320,3584]{1,0:T(8,128)(2,1)}, u32[]{:S(2)}, u32[]{:S(2)}) collective-permute-start(bf16[320,3584]{1,0:T(8,128)(2,1)} %bitcast.59), channel_id=1, source_target_pairs={{0,6},{2,0},{4,2},{6,4},{1,7},{3,1},{5,3},{7,5},{8,14},{10,8},{12,... | collective-permute-start | bytes 6881288 | tf_op jit(solution)/shard_map/ppermute | solution.py:18
  147.1 80.8 %collective-permute-start.13 = (bf16[320,3584]{1,0:T(8,128)(2,1)}, bf16[320,3584]{1,0:T(8,128)(2,1)}, u32[]{:S(2)}, u32[]{:S(2)}) collective-permute-start(bf16[320,3584]{1,0:T(8,128)(2,1)} %bitcast.60), channel_id=1, source_target_pairs={{0,2},{2,4},{4,6},{6,0},{1,3},{3,5},{5,7},{7,1},{8,10},{10,12},{12... | collective-permute-start | bytes 6881288 | tf_op jit(solution)/shard_map/ppermute | solution.py:18
  178.8 66.6 %collective-permute-start.17 = (bf16[128,3584]{1,0:T(8,128)(2,1)}, bf16[128,3584]{1,0:T(8,128)(2,1)}, u32[]{:S(2)}, u32[]{:S(2)}) collective-permute-start(bf16[128,3584]{1,0:T(8,128)(2,1)} %get-tuple-element.47), channel_id=1, source_target_pairs={{0,6},{2,0},{4,2},{6,4},{1,7},{3,1},{5,3},{7,5},{8,14},{10,8},{12,... | collective-permute-start | bytes 2752520 | tf_op jit(solution)/shard_map/ppermute | solution.py:22
  178.9 68.6 %collective-permute-start.16 = (bf16[128,3584]{1,0:T(8,128)(2,1)}, bf16[128,3584]{1,0:T(8,128)(2,1)}, u32[]{:S(2)}, u32[]{:S(2)}) collective-permute-start(bf16[128,3584]{1,0:T(8,128)(2,1)} %get-tuple-element.46), channel_id=1, source_target_pairs={{0,2},{2,4},{4,6},{6,0},{1,3},{3,5},{5,7},{7,1},{8,10},{10,12},{12... | collective-permute-start | bytes 2752520 | tf_op jit(solution)/shard_map/ppermute | solution.py:22
  197.9 75.4 %all-to-all-start.2 = ((bf16[16,40,1792]{2,1,0:T(8,128)(2,1)}), bf16[16,40,1792]{2,1,0:T(8,128)(2,1)}, u32[]{:S(2)}, u32[]{:S(2)}) async-start(bf16[16,40,1792]{2,1,0:T(8,128)(2,1)} %bitcast.63), calls=%async_computation.2 | async-start | bytes 4587520 | tf_op jit(solution)/shard_map/all_to_all | solution.py:30
  250.7 28.5 %collective-permute-start.18 = (bf16[320,1792]{1,0:T(8,128)(2,1)}, bf16[320,1792]{1,0:T(8,128)(2,1)}, u32[]{:S(2)}, u32[]{:S(2)}) collective-permute-start(bf16[320,1792]{1,0:T(8,128)(2,1)} %get-tuple-element.76), channel_id=1, source_target_pairs={{0,2},{2,4},{4,6},{6,0},{1,3},{3,5},{5,7},{7,1},{8,10},{10,12},{12... | collective-permute-start | bytes 3440648 | tf_op jit(solution)/shard_map/ppermute | solution.py:22
  250.7 28.5 %collective-permute-start.19 = (bf16[320,1792]{1,0:T(8,128)(2,1)}, bf16[320,1792]{1,0:T(8,128)(2,1)}, u32[]{:S(2)}, u32[]{:S(2)}) collective-permute-start(bf16[320,1792]{1,0:T(8,128)(2,1)} %get-tuple-element.77), channel_id=1, source_target_pairs={{0,6},{2,0},{4,2},{6,4},{1,7},{3,1},{5,3},{7,5},{8,14},{10,8},{12,... | collective-permute-start | bytes 3440648 | tf_op jit(solution)/shard_map/ppermute | solution.py:22
  276.5 26.6 %collective-permute-start.20 = (bf16[320,1792]{1,0:T(8,128)(2,1)}, bf16[320,1792]{1,0:T(8,128)(2,1)}, u32[]{:S(2)}, u32[]{:S(2)}) collective-permute-start(bf16[320,1792]{1,0:T(8,128)(2,1)} %get-tuple-element.78), channel_id=1, source_target_pairs={{0,2},{2,4},{4,6},{6,0},{1,3},{3,5},{5,7},{7,1},{8,10},{10,12},{12... | collective-permute-start | bytes 3440648 | tf_op jit(solution)/shard_map/ppermute | solution.py:22
  276.5 26.6 %collective-permute-start.21 = (bf16[320,1792]{1,0:T(8,128)(2,1)}, bf16[320,1792]{1,0:T(8,128)(2,1)}, u32[]{:S(2)}, u32[]{:S(2)}) collective-permute-start(bf16[320,1792]{1,0:T(8,128)(2,1)} %get-tuple-element.79), channel_id=1, source_target_pairs={{0,6},{2,0},{4,2},{6,4},{1,7},{3,1},{5,3},{7,5},{8,14},{10,8},{12,... | collective-permute-start | bytes 3440648 | tf_op jit(solution)/shard_map/ppermute | solution.py:22
  281.0 13.5 %all-to-all-start.3 = ((f32[16,1,80]{2,1,0:T(1,128)}), f32[16,1,80]{2,1,0:T(1,128)S(1)}, u32[]{:S(2)}, u32[]{:S(2)}) async-start(f32[16,1,80]{2,1,0:T(1,128)} %bitcast.23), calls=%async_computation.3 | async-start | bytes 16384 | tf_op jit(solution)/shard_map/all_to_all | solution.py:30
  295.8 22.1 %collective-permute-start.22 = (f32[16,20]{1,0:T(8,128)S(1)}, f32[16,20]{1,0:T(8,128)S(1)}, u32[]{:S(2)}, u32[]{:S(2)}) collective-permute-start(f32[16,20]{1,0:T(8,128)S(1)} %bitcast.67), channel_id=1, source_target_pairs={{0,2},{2,4},{4,6},{6,0},{1,3},{3,5},{5,7},{7,1},{8,10},{10,12},{12... | collective-permute-start | bytes 3848 | tf_op jit(solution)/shard_map/ppermute | solution.py:22
  295.9 22.0 %collective-permute-start.23 = (f32[16,20]{1,0:T(8,128)S(1)}, f32[16,20]{1,0:T(8,128)S(1)}, u32[]{:S(2)}, u32[]{:S(2)}) collective-permute-start(f32[16,20]{1,0:T(8,128)S(1)} %bitcast.66), channel_id=1, source_target_pairs={{0,4},{2,6},{4,0},{6,2},{1,5},{3,7},{5,1},{7,3},{8,12},{10,14},{12... | collective-permute-start | bytes 3848 | tf_op jit(solution)/shard_map/ppermute | solution.py:22
  298.3 6.7 %copy-start.14 = (bf16[640,1792]{1,0:T(8,128)(2,1)S(1)}, bf16[640,1792]{1,0:T(8,128)(2,1)}, u32[]{:S(2)}) copy-start(bf16[640,1792]{1,0:T(8,128)(2,1)} %get-tuple-element.29) | copy-start | bytes 6881284
  298.3 19.6 %collective-permute-start.24 = (f32[16,20]{1,0:T(8,128)S(1)}, f32[16,20]{1,0:T(8,128)S(1)}, u32[]{:S(2)}, u32[]{:S(2)}) collective-permute-start(f32[16,20]{1,0:T(8,128)S(1)} %bitcast.65), channel_id=1, source_target_pairs={{0,6},{2,0},{4,2},{6,4},{1,7},{3,1},{5,3},{7,5},{8,14},{10,8},{12,... | collective-permute-start | bytes 3848 | tf_op jit(solution)/shard_map/ppermute | solution.py:22
  307.0 34.1 %all-to-all-start.4 = ((bf16[16,40,1792]{2,1,0:T(8,128)(2,1)}), bf16[16,40,1792]{2,1,0:T(8,128)(2,1)S(1)}, u32[]{:S(2)}, u32[]{:S(2)}) async-start(bf16[16,40,1792]{2,1,0:T(8,128)(2,1)} %bitcast.29), calls=%async_computation.4 | async-start | bytes 4587520 | tf_op jit(solution)/shard_map/all_to_all | solution.py:30
  313.9 4.3 %copy-start.26 = (f32[128,2]{0,1:T(2,128)S(1)}, f32[128,2]{0,1:T(2,128)}, u32[]{:S(2)}) copy-start(f32[128,2]{0,1:T(2,128)} %select_reduce_fusion.6) | copy-start | bytes 3076
  313.9 4.3 %copy-start.9 = (bf16[128,3584]{1,0:T(8,128)(2,1)S(1)}, bf16[128,3584]{1,0:T(8,128)(2,1)}, u32[]{:S(2)}) copy-start(bf16[128,3584]{1,0:T(8,128)(2,1)} %copy-done.7) | copy-start | bytes 2752516
  313.9 4.3 %copy-start.21 = (pred[128,2,16]{0,2,1:T(8,128)(4,1)S(1)}, pred[128,2,16]{0,2,1:T(8,128)(4,1)}, u32[]{:S(2)}) copy-start(pred[128,2,16]{0,2,1:T(8,128)(4,1)} %iota_compare_fusion.15) | copy-start | bytes 12292
  316.8 5.5 %copy-start.20 = (s32[128,2]{0,1:T(2,128)S(1)}, s32[128,2]{0,1:T(2,128)}, u32[]{:S(2)}) copy-start(s32[128,2]{0,1:T(2,128)} %copy-done.19) | copy-start | bytes 3076
  316.8 5.5 %copy-start.23 = (s32[128,2]{0,1:T(2,128)S(1)}, s32[128,2]{0,1:T(2,128)}, u32[]{:S(2)}) copy-start(s32[128,2]{0,1:T(2,128)} %copy-done.22) | copy-start | bytes 3076
  316.8 25.3 %collective-permute-start.25 = (bf16[128,3584]{1,0:T(8,128)(2,1)}, bf16[128,3584]{1,0:T(8,128)(2,1)}, u32[]{:S(2)}, u32[]{:S(2)}) collective-permute-start(bf16[128,3584]{1,0:T(8,128)(2,1)} %fusion.13), channel_id=1, source_target_pairs={{0,4},{2,6},{4,0},{6,2},{1,5},{3,7},{5,1},{7,3},{8,12},{10,14},{12... | collective-permute-start | bytes 2752520 | tf_op jit(solution)/shard_map/ppermute | solution.py:22
  343.7 4.3 %copy-start.15 = (f32[16,3584]{1,0:T(8,128)S(1)}, f32[16,3584]{1,0:T(8,128)}, u32[]{:S(2)}) copy-start(f32[16,3584]{1,0:T(8,128)} %fusion.59) | copy-start | bytes 688132
  348.0 30.1 %copy-start.12 = (bf16[128,3584]{1,0:T(8,128)(2,1)S(1)}, bf16[128,3584]{1,0:T(8,128)(2,1)}, u32[]{:S(2)}) copy-start(bf16[128,3584]{1,0:T(8,128)(2,1)} %param.12) | copy-start | bytes 2752516
  349.2 23.0 %all-to-all-start.5 = ((f32[128,1,476]{2,1,0:T(1,128)}), f32[128,1,476]{2,1,0:T(1,128)S(1)}, u32[]{:S(2)}, u32[]{:S(2)}) async-start(f32[128,1,476]{2,1,0:T(1,128)} %all_to_all.64), calls=%async_computation.5 | async-start | bytes 524288 | tf_op jit(solution)/shard_map/all_to_all | solution.py:30
  373.3 15.5 %all-to-all-start.6 = ((f32[128,1,476]{2,1,0:T(1,128)}), f32[128,1,476]{2,1,0:T(1,128)S(1)}, u32[]{:S(2)}, u32[]{:S(2)}) async-start(f32[128,1,476]{2,1,0:T(1,128)} %broadcast_in_dim.95), calls=%async_computation.6 | async-start | bytes 524288 | tf_op jit(solution)/shard_map/all_to_all | solution.py:30
  (13 other events, 20.0 us)
where the time goes:
time: 399 us; the launch traced here: 392 us
  waiting for transfers between devices  119 us (30%)
  Pallas kernels  103 us (26%)
  starting transfers between devices  99.4 us (25%)
  local copies, waits for them, and re-layouts  30.9 us (8%)
  other arithmetic  26.2 us (7%)
  matrix products  10.7 us (3%)
    pallas_call x5, Pallas kernels, hidden_grads(): pl.pallas_call(lambda *refs: hidden_kernel(lengths, mixed, *refs), grid=(...  91.9 us
    all_to_all x7, waiting for transfers between devices, over(): return lax.all_to_all(value, axes, split_axis=0, concat_axis=0, tiled=True)  85.1 us
    all_to_all x7, starting transfers between devices, over(): return lax.all_to_all(value, axes, split_axis=0, concat_axis=0, tiled=True)  57 us
    ppermute x10, waiting for transfers between devices, receive_from(): lax.ppermute(value, 'y', [(i, (i - k) % PEERS) for i in range(PEERS)])  27.2 us
    ppermute x10, starting transfers between devices, receive_from(): lax.ppermute(value, 'y', [(i, (i - k) % PEERS) for i in range(PEERS)])  24.4 us
    pallas_call x2, Pallas kernels, pick_rows(): pl.pallas_call(pick_kernel, grid=(width // block,), in_specs=[pl.BlockSpe...  11.6 us
    ppermute x10, starting transfers between devices, send_to(): lax.ppermute(value, 'y', [(i, (i + k) % PEERS) for i in range(PEERS)])  11.2 us
  transfers between devices with their start and end apart: 33, of which 11 were waited for; matrix products, arithmetic and copies ran while one was open for 13% of the time, Pallas kernels for 26%

commit v1 on v0

--- a/solution.py
+++ b/solution.py
@@ -302,7 +302,9 @@
     dense = weight_pieces(*(after(v, own_send) for v in (dense_gate, dense_up, dense_down)))
     chunk = everything // 2
     parts = [own[:chunk], own[chunk:]]
-    near = [{k: receive_from(part, k) for k in (1, 3)} for part in parts]
+    near = [{k: receive_from(parts[0], k) for k in (1, 3)}]
+    second = after(parts[1], near[0][1], near[0][3])
+    near.append({k: receive_from(second, k) for k in (1, 3)})
     far = over(pick_for(after(far_pair, *parts), far_index))
     table = shuffle_table(cap, experts // 2)
     tables = (table, table.T)
@@ -317,24 +319,23 @@
         ],
         dense,
     )
-    far_into, far_joint = hidden_grads([(after(far, dense_part),)], expert, tables)
-    far_back = over(far_into)
     near_into = [None, None]
     near_joint = [None, None]
     near_into[0], near_joint[0] = hidden_grads(
-        [(after(near[0][1], far_into),), (near[0][3],)], expert, tables
-    )
+        [(after(near[0][1], dense_part),), (near[0][3],)], expert, tables
+    )
+    far_into, far_joint = hidden_grads([(after(far, near_into[0]),)], expert, tables)
+    far_back = over(far_into)
     near_into[1], near_joint[1] = hidden_grads(
-        [(after(near[1][1], near_into[0]),), (near[1][3],)], expert, tables
-    )
-    near_into[1] = after(near_into[1], far_back)
-    arrived = (near[1][1], near[1][3])
-    home1 = send_to(after(dense_part[tok : 2 * tok], *arrived), 1)
-    home3 = send_to(after(dense_part[3 * tok :], *arrived), 3)
-    near_back = []
-    for i in (0, 1):
-        first = after(near_into[i], home1, home3) if i == 0 else near_into[i]
-        near_back.append(send_to(first[:chunk], 1).astype(F32) + send_to(first[chunk:], 3).astype(F32))
+        [(after(near[1][1], far_into),), (near[1][3],)], expert, tables
+    )
+    first = after(near_into[0], near[1][1], near[1][3])
+    first_back = (send_to(first[:chunk], 1), send_to(first[chunk:], 3))
+    home1 = send_to(after(dense_part[tok : 2 * tok], *first_back), 1)
+    home3 = send_to(after(dense_part[3 * tok :], *first_back), 3)
+    other = after(near_into[1], far_back, home1, home3)
+    other_back = (send_to(other[:chunk], 1), send_to(other[chunk:], 3))
+    near_back = [v[0].astype(F32) + v[1].astype(F32) for v in (first_back, other_back)]
 
     joints = jnp.stack(
         [

time: 399 us -> 420 us (1.053)
  waiting for transfers between devices: 119 us -> 133 us
  starting transfers between devices: 99.4 us -> 108 us
    ppermute x10, waiting for transfers between devices: 6.78 us -> 19.5 us  [send_to(): lax.ppermute(value, 'y', [(i, (i + k) % PEERS) for i in range(PEERS)])]
    all_to_all x7, starting transfers between devices: 57 us -> 63.1 us  [over(): return lax.all_to_all(value, axes, split_axis=0, concat_axis=0, tiled=True)]
  transfers between devices with their start and end apart: 33 -> 33, of which waited for: 11 -> 9; matrix products, arithmetic and copies ran while one was open for 13% -> 11% of each run, Pallas kernels for 26% -> 25%
where the time goes in v1:
time: 420 us; the launch traced here: 412 us
  waiting for transfers between devices  133 us (32%)
  starting transfers between devices  108 us (26%)
  Pallas kernels  104 us (25%)
  local copies, waits for them, and re-layouts  31.3 us (7%)
  other arithmetic  23.8 us (6%)
  matrix products  11.3 us (3%)
    pallas_call x5, Pallas kernels, hidden_grads(): pl.pallas_call(lambda *refs: hidden_kernel(lengths, mixed, *refs), grid=(...  91.9 us
    all_to_all x7, waiting for transfers between devices, over(): return lax.all_to_all(value, axes, split_axis=0, concat_axis=0, tiled=True)  84.1 us
    all_to_all x7, starting transfers between devices, over(): return lax.all_to_all(value, axes, split_axis=0, concat_axis=0, tiled=True)  63.1 us
    ppermute x10, waiting for transfers between devices, receive_from(): lax.ppermute(value, 'y', [(i, (i - k) % PEERS) for i in range(PEERS)])  29.3 us
    ppermute x10, starting transfers between devices, receive_from(): lax.ppermute(value, 'y', [(i, (i - k) % PEERS) for i in range(PEERS)])  24.8 us
    ppermute x10, waiting for transfers between devices, send_to(): lax.ppermute(value, 'y', [(i, (i + k) % PEERS) for i in range(PEERS)])  19.5 us
    ppermute x10, starting transfers between devices, send_to(): lax.ppermute(value, 'y', [(i, (i + k) % PEERS) for i in range(PEERS)])  13.1 us
    pallas_call x2, Pallas kernels, pick_rows(): pl.pallas_call(pick_kernel, grid=(width // block,), in_specs=[pl.BlockSpe...  11.6 us
  transfers between devices with their start and end apart: 33, of which 9 were waited for; matrix products, arithmetic and copies ran while one was open for 11% of the time, Pallas kernels for 25%

profile of v1, /device:TPU:1, one launch (start us, length us, event | category | flops | bytes accessed | tf_op | source)
XLA Modules:
  0.0 412.1 jit_solution(1629967340841420027)
XLA Ops:
  0.7 2.2 fusion.84
  2.9 3.6 collective-permute-start
  7.5 1.9 collective-permute-start.4
  11.2 1.6 pad_maximum_fusion.rows.refs_0_
  13.1 4.9 %shard_map.130 = bf16[640,3584]{1,0:T(8,128)(2,1)} custom-call(bf16[640,256]{1,0:T(8,128)(2,1)S(1)} %fusion.47.table, bf16[256,3584]{1,0:T(8,128)(2,1)S(1)} %pad_maximum_fusion.rows.refs_0_), custom_call_target="tpu_custom_call" | custom-call | flops 1174405120 | bytes 6422528 | tf_op jit(solution)/shard_map/pallas_call | solution.py:206
  19.0 7.7 %all-to-all-start = ((bf16[16,40,3584]{2,1,0:T(8,128)(2,1)}), bf16[16,40,3584]{2,1,0:T(8,128)(2,1)}, u32[]{:S(2)}, u32[]{:S(2)}) async-start(bf16[16,40,3584]{2,1,0:T(8,128)(2,1)} %bitcast.57), calls=%async_computation | async-start | bytes 9175040 | tf_op jit(solution)/shard_map/all_to_all | solution.py:30
  27.7 2.4 collective-permute-start.5
  30.1 52.8 %all-to-all-done = bf16[16,40,3584]{2,1,0:T(8,128)(2,1)} async-done(((bf16[16,40,3584]{2,1,0:T(8,128)(2,1)}), bf16[16,40,3584]{2,1,0:T(8,128)(2,1)}, u32[]{:S(2)}, u32[]{:S(2)}) %all-to-all-start) | async-done | bytes 4587552 | tf_op jit(solution)/shard_map/all_to_all | solution.py:30
  82.8 4.7 %fusion.78 = (bf16[8,40,3584]{2,1,0:T(8,128)(2,1)}, bf16[8,40,3584]{2,1,0:T(8,128)(2,1)}) fusion(bf16[16,40,3584]{2,1,0:T(8,128)(2,1)} %all-to-all-done), kind=kLoop, calls=%fused_computation.156 | loop fusion | bytes 9175040 | tf_op jit(solution)/shard_map/slice | solution.py:304
  87.6 6.9 %collective-permute-start.12 = (bf16[320,3584]{1,0:T(8,128)(2,1)}, bf16[320,3584]{1,0:T(8,128)(2,1)}, u32[]{:S(2)}, u32[]{:S(2)}) collective-permute-start(bf16[320,3584]{1,0:T(8,128)(2,1)} %bitcast.12), channel_id=1, source_target_pairs={{0,6},{2,0},{4,2},{6,4},{1,7},{3,1},{5,3},{7,5},{8,14},{10,8},{12,... | collective-permute-start | bytes 6881288 | tf_op jit(solution)/shard_map/ppermute | solution.py:18
  94.4 7.9 %collective-permute-start.13 = (bf16[320,3584]{1,0:T(8,128)(2,1)}, bf16[320,3584]{1,0:T(8,128)(2,1)}, u32[]{:S(2)}, u32[]{:S(2)}) collective-permute-start(bf16[320,3584]{1,0:T(8,128)(2,1)} %bitcast.12), channel_id=1, source_target_pairs={{0,2},{2,4},{4,6},{6,0},{1,3},{3,5},{5,7},{7,1},{8,10},{10,12},{12... | collective-permute-start | bytes 6881288 | tf_op jit(solution)/shard_map/ppermute | solution.py:18
  108.1 6.7 %shard_map.134 = bf16[640,3584]{1,0:T(8,128)(2,1)} custom-call(bf16[640,256]{1,0:T(8,128)(2,1)S(1)} %fusion.46.table, bf16[256,3584]{1,0:T(8,128)(2,1)} %collective-permute-done.7.refs_3_.rows), custom_call_target="tpu_custom_call" | custom-call | flops 1174405120 | bytes 6422528 | tf_op jit(solution)/shard_map/pallas_call | solution.py:206
  114.8 8.8 %all-to-all-start.1 = ((bf16[16,40,3584]{2,1,0:T(8,128)(2,1)}), bf16[16,40,3584]{2,1,0:T(8,128)(2,1)}, u32[]{:S(2)}, u32[]{:S(2)}) async-start(bf16[16,40,3584]{2,1,0:T(8,128)(2,1)} %bitcast.56), calls=%async_computation.1 | async-start | bytes 9175040 | tf_op jit(solution)/shard_map/all_to_all | solution.py:30
  124.4 2.6 collective-permute-start.10
  128.8 2.0 fusion.24
  130.8 19.3 %collective-permute-done.12.refs_0_ = bf16[320,3584]{1,0:T(8,128)(2,1)} collective-permute-done((bf16[320,3584]{1,0:T(8,128)(2,1)}, bf16[320,3584]{1,0:T(8,128)(2,1)}, u32[]{:S(2)}, u32[]{:S(2)}) %collective-permute-start.12) | collective-permute-done | bytes 2293792 | tf_op jit(solution)/shard_map/ppermute | solution.py:18
  150.1 1.7 collective-permute-start.8
  152.0 17.3 %shard_map.131 = (bf16[640,1792]{1,0:T(8,128)(2,1)}, f32[320,128]{1,0:T(8,128)S(1)}) custom-call(bf16[640,3584]{1,0:T(8,128)(2,1)} %bitcast.7.refs_0_, bf16[304,3584]{1,0:T(8,128)(2,1)S(1)} %bitcast.52, bf16[304,3584]{1,0:T(8,128)(2,1)} %collective-permute-done.2.refs_2_.refs_3_, bf16[304,3584]{1,0:T(8,128)(2,1)} %bitcast.75, ...), custom_call_target="tpu_custom_call" | custom-call | flops 7340032000 | bytes 20643840 | tf_op jit(solution)/shard_map/pallas_call | solution.py:168
  169.6 9.0 %collective-permute-done.6.refs_2_ = bf16[192,3584]{1,0:T(8,128)(2,1)S(1)} collective-permute-done((bf16[192,3584]{1,0:T(8,128)(2,1)}, bf16[192,3584]{1,0:T(8,128)(2,1)S(1)}, u32[]{:S(2)}, u32[]{:S(2)}) %collective-permute-start.6) | collective-permute-done | bytes 1376288 | tf_op jit(solution)/shard_map/ppermute | solution.py:18
  180.6 21.9 %shard_map.132 = (bf16[512,3584]{1,0:T(8,128)(2,1)}, f32[512,128]{1,0:T(8,128)}) custom-call(bf16[256,3584]{1,0:T(8,128)(2,1)} %copy-done.1, bf16[64,3584]{1,0:T(8,128)(2,1)S(1)} %collective-permute-done.refs_1_, bf16[192,3584]{1,0:T(8,128)(2,1)S(1)} %collective-permute-done.6.refs_2_, bf16[256,3584]{1,0:T(8,128)(2,1)} %collective-permute-done.7.refs_3_.rows, ...), custom_call_target="tpu_custom_call" | custom-call | flops 11744051200 | bytes 24772608 | tf_op jit(solution)/shard_map/pallas_call | solution.py:168
  202.5 17.5 %shard_map.133 = (bf16[640,1792]{1,0:T(8,128)(2,1)}, f32[320,128]{1,0:T(8,128)S(1)}) custom-call(bf16[320,3584]{1,0:T(8,128)(2,1)} %collective-permute-done.12.refs_0_, bf16[320,3584]{1,0:T(8,128)(2,1)} %collective-permute-done.13.refs_1_, bf16[304,3584]{1,0:T(8,128)(2,1)S(1)} %bitcast.53, bf16[304,3584]{1,0:T(8,128)(2,1)} %collective-permute-done.2.refs_2_.refs_3_, ...), custom_call_target="tpu_custom_call" | custom-call | flops 7340032000 | bytes 20643840 | tf_op jit(solution)/shard_map/pallas_call | solution.py:168
  220.0 1.6 copy-done.4
  221.6 17.5 %shard_map.135 = (bf16[640,1792]{1,0:T(8,128)(2,1)}, f32[320,128]{1,0:T(8,128)S(1)}) custom-call(bf16[640,3584]{1,0:T(8,128)(2,1)} %bitcast.19.refs_0_, bf16[304,3584]{1,0:T(8,128)(2,1)S(1)} %bitcast.54, bf16[304,3584]{1,0:T(8,128)(2,1)} %collective-permute-done.2.refs_2_.refs_3_, bf16[304,3584]{1,0:T(8,128)(2,1)} %bitcast.77, ...), custom_call_target="tpu_custom_call" | custom-call | flops 7340032000 | bytes 20643840 | tf_op jit(solution)/shard_map/pallas_call | solution.py:168
  239.2 10.2 %all-to-all-start.2 = ((bf16[16,40,1792]{2,1,0:T(8,128)(2,1)}), bf16[16,40,1792]{2,1,0:T(8,128)(2,1)}, u32[]{:S(2)}, u32[]{:S(2)}) async-start(bf16[16,40,1792]{2,1,0:T(8,128)(2,1)} %bitcast.61), calls=%async_computation.2 | async-start | bytes 4587520 | tf_op jit(solution)/shard_map/all_to_all | solution.py:30
  249.4 3.3 fusion.81
  253.7 1.7 collective-permute-start.17
  257.3 19.5 %collective-permute-done.16 = bf16[320,1792]{1,0:T(8,128)(2,1)S(1)} collective-permute-done((bf16[320,1792]{1,0:T(8,128)(2,1)}, bf16[320,1792]{1,0:T(8,128)(2,1)S(1)}, u32[]{:S(2)}, u32[]{:S(2)}) %collective-permute-start.16) | collective-permute-done | bytes 1146912 | tf_op jit(solution)/shard_map/ppermute | solution.py:22
  276.7 2.4 collective-permute-start.19
  280.8 17.6 %shard_map.136 = (bf16[640,1792]{1,0:T(8,128)(2,1)}, f32[320,128]{1,0:T(8,128)S(1)}) custom-call(bf16[320,3584]{1,0:T(8,128)(2,1)} %collective-permute-done.14.refs_0_, bf16[320,3584]{1,0:T(8,128)(2,1)} %collective-permute-done.15.refs_1_, bf16[304,3584]{1,0:T(8,128)(2,1)S(1)} %bitcast.55, bf16[304,3584]{1,0:T(8,128)(2,1)} %collective-permute-done.2.refs_2_.refs_3_, ...), custom_call_target="tpu_custom_call" | custom-call | flops 7340032000 | bytes 20643840 | tf_op jit(solution)/shard_map/pallas_call | solution.py:168
  299.5 3.5 fusion.80
  303.1 2.6 collective-permute-start.21
  307.2 6.6 %all-to-all-start.3 = ((f32[16,1,80]{2,1,0:T(1,128)}), f32[16,1,80]{2,1,0:T(1,128)S(1)}, u32[]{:S(2)}, u32[]{:S(2)}) async-start(f32[16,1,80]{2,1,0:T(1,128)} %bitcast.23), calls=%async_computation.3 | async-start | bytes 16384 | tf_op jit(solution)/shard_map/all_to_all | solution.py:30
  313.8 2.5 fusion.48
  317.8 2.4 all-to-all-done.3
  321.5 2.6 collective-permute-start.23
  324.8 1.9 convert_add_fusion
  326.7 2.0 fusion
  328.7 5.6 %all-to-all-start.4 = ((bf16[16,40,1792]{2,1,0:T(8,128)(2,1)}), bf16[16,40,1792]{2,1,0:T(8,128)(2,1)S(1)}, u32[]{:S(2)}, u32[]{:S(2)}) async-start(bf16[16,40,1792]{2,1,0:T(8,128)(2,1)} %bitcast.29), calls=%async_computation.4 | async-start | bytes 4587520 | tf_op jit(solution)/shard_map/all_to_all | solution.py:30
  334.3 2.9 fusion.13
  337.2 2.1 collective-permute-start.25
  340.7 2.9 fusion.60
  343.8 10.5 %all-to-all-done.4 = bf16[16,40,1792]{2,1,0:T(8,128)(2,1)S(1)} async-done(((bf16[16,40,1792]{2,1,0:T(8,128)(2,1)}), bf16[16,40,1792]{2,1,0:T(8,128)(2,1)S(1)}, u32[]{:S(2)}, u32[]{:S(2)}) %all-to-all-start.4) | async-done | bytes 2293792 | tf_op jit(solution)/shard_map/all_to_all | solution.py:30
  357.3 4.0 fusion.12
  362.4 19.6 %all-to-all-start.5 = ((f32[128,1,476]{2,1,0:T(1,128)}), f32[128,1,476]{2,1,0:T(1,128)S(1)}, u32[]{:S(2)}, u32[]{:S(2)}) async-start(f32[128,1,476]{2,1,0:T(1,128)} %all_to_all.64), calls=%async_computation.5 | async-start | bytes 524288 | tf_op jit(solution)/shard_map/all_to_all | solution.py:30
  382.0 10.8 %all-to-all-done.5 = f32[128,1,476]{2,1,0:T(1,128)S(1)} async-done(((f32[128,1,476]{2,1,0:T(1,128)}), f32[128,1,476]{2,1,0:T(1,128)S(1)}, u32[]{:S(2)}, u32[]{:S(2)}) %all-to-all-start.5) | async-done | bytes 243744 | tf_op jit(solution)/shard_map/all_to_all | solution.py:30
  393.9 4.8 %all-to-all-start.6 = ((f32[128,1,476]{2,1,0:T(1,128)}), f32[128,1,476]{2,1,0:T(1,128)S(1)}, u32[]{:S(2)}, u32[]{:S(2)}) async-start(f32[128,1,476]{2,1,0:T(1,128)} %broadcast_in_dim.95), calls=%async_computation.6 | async-start | bytes 524288 | tf_op jit(solution)/shard_map/all_to_all | solution.py:30
  398.6 3.1 fusion.8
  401.7 7.7 %all-to-all-done.6 = f32[128,1,476]{2,1,0:T(1,128)S(1)} async-done(((f32[128,1,476]{2,1,0:T(1,128)}), f32[128,1,476]{2,1,0:T(1,128)S(1)}, u32[]{:S(2)}, u32[]{:S(2)}) %all-to-all-start.6) | async-done | bytes 243744 | tf_op jit(solution)/shard_map/all_to_all | solution.py:30
  (178 shorter events, 35.2 us)
Async XLA Ops:
  0.6 123.0 %copy-start = (f32[3584,16]{0,1:T(8,128)S(1)}, f32[3584,16]{0,1:T(8,128)}, u32[]{:S(2)}) copy-start(f32[3584,16]{0,1:T(8,128)} %param.14) | copy-start | bytes 688132
  0.6 6.8 %copy-start.22 = (s32[128,2]{0,1:T(2,128)S(1)}, s32[128,2]{0,1:T(2,128)}, u32[]{:S(2)}) copy-start(s32[128,2]{0,1:T(2,128)} %param.21) | copy-start | bytes 3076
  0.7 10.0 %copy-start.9 = (bf16[128,3584]{1,0:T(8,128)(2,1)S(1)}, bf16[128,3584]{1,0:T(8,128)(2,1)}, u32[]{:S(2)}) copy-start(bf16[128,3584]{1,0:T(8,128)(2,1)} %param.11) | copy-start | bytes 2752516
  0.7 10.3 %copy-start.21 = (f32[3584]{0:T(1024)S(1)}, f32[3584]{0:T(1024)}, u32[]{:S(2)}) copy-start(f32[3584]{0:T(1024)} %param.13) | copy-start | bytes 43012
  2.9 15.2 %collective-permute-start = (bf16[64,3584]{1,0:T(8,128)(2,1)}, bf16[64,3584]{1,0:T(8,128)(2,1)S(1)}, u32[]{:S(2)}, u32[]{:S(2)}) collective-permute-start(bf16[64,3584]{1,0:T(8,128)(2,1)} %get-tuple-element.87), channel_id=1, source_target_pairs={{0,6},{2,0},{4,2},{6,4},{1,7},{3,1},{5,3},{7,5},{8,14},{10,8},{12,... | collective-permute-start | bytes 1376264 | tf_op jit(solution)/shard_map/ppermute | solution.py:18
  6.5 12.5 %collective-permute-start.1 = (bf16[64,3584]{1,0:T(8,128)(2,1)}, bf16[64,3584]{1,0:T(8,128)(2,1)S(1)}, u32[]{:S(2)}, u32[]{:S(2)}) collective-permute-start(bf16[64,3584]{1,0:T(8,128)(2,1)} %get-tuple-element.87), channel_id=1, source_target_pairs={{0,2},{2,4},{4,6},{6,0},{1,3},{3,5},{5,7},{7,1},{8,10},{10,12},{12... | collective-permute-start | bytes 1376264 | tf_op jit(solution)/shard_map/ppermute | solution.py:18
  6.5 12.5 %collective-permute-start.2 = (bf16[304,3584]{1,0:T(8,128)(2,1)}, bf16[304,3584]{1,0:T(8,128)(2,1)}, u32[]{:S(2)}, u32[]{:S(2)}) collective-permute-start(bf16[304,3584]{1,0:T(8,128)(2,1)} %bitcast.51), channel_id=1, source_target_pairs={{0,1},{1,0},{2,3},{3,2},{4,5},{5,4},{6,7},{7,6},{8,9},{9,8},{10,11... | collective-permute-start | bytes 6537224 | tf_op jit(solution)/shard_map/ppermute | solution.py:26
  7.5 11.5 %collective-permute-start.3 = (bf16[304,3584]{1,0:T(8,128)(2,1)}, bf16[304,3584]{1,0:T(8,128)(2,1)}, u32[]{:S(2)}, u32[]{:S(2)}) collective-permute-start(bf16[304,3584]{1,0:T(8,128)(2,1)} %bitcast.74), channel_id=1, source_target_pairs={{0,1},{1,0},{2,3},{3,2},{4,5},{5,4},{6,7},{7,6},{8,9},{9,8},{10,11... | collective-permute-start | bytes 6537224 | tf_op jit(solution)/shard_map/ppermute | solution.py:26
  7.5 10.6 %collective-permute-start.4 = (s32[128,2]{0,1:T(2,128)S(1)}, s32[128,2]{0,1:T(2,128)S(1)}, u32[]{:S(2)}, u32[]{:S(2)}) collective-permute-start(s32[128,2]{0,1:T(2,128)S(1)} %copy-done.22), channel_id=1, source_target_pairs={{0,4},{2,6},{4,0},{6,2},{1,5},{3,7},{5,1},{7,3},{8,12},{10,14},{12... | collective-permute-start | bytes 3080 | tf_op jit(solution)/shard_map/ppermute | solution.py:18
  12.9 13.8 %copy-start.1 = (bf16[256,3584]{1,0:T(8,128)(2,1)}, bf16[256,3584]{1,0:T(8,128)(2,1)S(1)}, u32[]{:S(2)}) copy-start(bf16[256,3584]{1,0:T(8,128)(2,1)S(1)} %pad_maximum_fusion.rows.refs_0_) | copy-start | bytes 5505028
  19.0 63.8 %all-to-all-start = ((bf16[16,40,3584]{2,1,0:T(8,128)(2,1)}), bf16[16,40,3584]{2,1,0:T(8,128)(2,1)}, u32[]{:S(2)}, u32[]{:S(2)}) async-start(bf16[16,40,3584]{2,1,0:T(8,128)(2,1)} %bitcast.57), calls=%async_computation | async-start | bytes 9175040 | tf_op jit(solution)/shard_map/all_to_all | solution.py:30
  26.7 81.5 %collective-permute-start.7 = (bf16[256,3584]{1,0:T(8,128)(2,1)S(1)}, bf16[256,3584]{1,0:T(8,128)(2,1)}, u32[]{:S(2)}, u32[]{:S(2)}) collective-permute-start(bf16[256,3584]{1,0:T(8,128)(2,1)S(1)} %pad_maximum_fusion.rows.refs_0_), channel_id=1, source_target_pairs={{0,4},{2,6},{4,0},{6,2},{1,5},{3,7},{5,1},{7,3},{8,12},{10,14},{12... | collective-permute-start | bytes 5505032 | tf_op jit(solution)/shard_map/ppermute | solution.py:18
  27.7 99.4 %collective-permute-start.5 = (bf16[304,3584]{1,0:T(8,128)(2,1)}, bf16[304,3584]{1,0:T(8,128)(2,1)}, u32[]{:S(2)}, u32[]{:S(2)}) collective-permute-start(bf16[304,3584]{1,0:T(8,128)(2,1)} %bitcast.79), channel_id=1, source_target_pairs={{0,1},{1,0},{2,3},{3,2},{4,5},{5,4},{6,7},{7,6},{8,9},{9,8},{10,11... | collective-permute-start | bytes 6537224 | tf_op jit(solution)/shard_map/ppermute | solution.py:26
  87.6 62.5 %collective-permute-start.12 = (bf16[320,3584]{1,0:T(8,128)(2,1)}, bf16[320,3584]{1,0:T(8,128)(2,1)}, u32[]{:S(2)}, u32[]{:S(2)}) collective-permute-start(bf16[320,3584]{1,0:T(8,128)(2,1)} %bitcast.12), channel_id=1, source_target_pairs={{0,6},{2,0},{4,2},{6,4},{1,7},{3,1},{5,3},{7,5},{8,14},{10,8},{12,... | collective-permute-start | bytes 6881288 | tf_op jit(solution)/shard_map/ppermute | solution.py:18
  94.4 55.6 %collective-permute-start.13 = (bf16[320,3584]{1,0:T(8,128)(2,1)}, bf16[320,3584]{1,0:T(8,128)(2,1)}, u32[]{:S(2)}, u32[]{:S(2)}) collective-permute-start(bf16[320,3584]{1,0:T(8,128)(2,1)} %bitcast.12), channel_id=1, source_target_pairs={{0,2},{2,4},{4,6},{6,0},{1,3},{3,5},{5,7},{7,1},{8,10},{10,12},{12... | collective-permute-start | bytes 6881288 | tf_op jit(solution)/shard_map/ppermute | solution.py:18
  114.8 8.8 %copy-start.23 = (s32[128,2]{0,1:T(2,128)S(1)}, s32[128,2]{0,1:T(2,128)}, u32[]{:S(2)}) copy-start(s32[128,2]{0,1:T(2,128)} %param.21) | copy-start | bytes 3076
  114.8 8.8 %copy-start.7 = (bf16[128,3584]{1,0:T(8,128)(2,1)S(1)}, bf16[128,3584]{1,0:T(8,128)(2,1)}, u32[]{:S(2)}) copy-start(bf16[128,3584]{1,0:T(8,128)(2,1)} %copy-done.6) | copy-start | bytes 2752516
  114.8 12.7 %copy-start.15 = (bf16[64,3584]{1,0:T(8,128)(2,1)S(1)}, bf16[64,3584]{1,0:T(8,128)(2,1)}, u32[]{:S(2)}) copy-start(bf16[64,3584]{1,0:T(8,128)(2,1)} %get-tuple-element.86) | copy-start | bytes 1376260
  114.8 105.2 %all-to-all-start.1 = ((bf16[16,40,3584]{2,1,0:T(8,128)(2,1)}), bf16[16,40,3584]{2,1,0:T(8,128)(2,1)}, u32[]{:S(2)}, u32[]{:S(2)}) async-start(bf16[16,40,3584]{2,1,0:T(8,128)(2,1)} %bitcast.56), calls=%async_computation.1 | async-start | bytes 9175040 | tf_op jit(solution)/shard_map/all_to_all | solution.py:30
  124.4 56.1 %collective-permute-start.10 = (bf16[304,3584]{1,0:T(8,128)(2,1)}, bf16[304,3584]{1,0:T(8,128)(2,1)}, u32[]{:S(2)}, u32[]{:S(2)}) collective-permute-start(bf16[304,3584]{1,0:T(8,128)(2,1)} %bitcast.72), channel_id=1, source_target_pairs={{0,1},{1,0},{2,3},{3,2},{4,5},{5,4},{6,7},{7,6},{8,9},{9,8},{10,11... | collective-permute-start | bytes 6537224 | tf_op jit(solution)/shard_map/ppermute | solution.py:26
  127.0 53.6 %collective-permute-start.11 = (bf16[304,3584]{1,0:T(8,128)(2,1)}, bf16[304,3584]{1,0:T(8,128)(2,1)}, u32[]{:S(2)}, u32[]{:S(2)}) collective-permute-start(bf16[304,3584]{1,0:T(8,128)(2,1)} %refs_10_), channel_id=1, source_target_pairs={{0,1},{1,0},{2,3},{3,2},{4,5},{5,4},{6,7},{7,6},{8,9},{9,8},{10,11... | collective-permute-start | bytes 6537224 | tf_op jit(solution)/shard_map/ppermute | solution.py:26
  127.1 53.5 %collective-permute-start.9 = (bf16[304,3584]{1,0:T(8,128)(2,1)}, bf16[304,3584]{1,0:T(8,128)(2,1)}, u32[]{:S(2)}, u32[]{:S(2)}) collective-permute-start(bf16[304,3584]{1,0:T(8,128)(2,1)} %bitcast.70), channel_id=1, source_target_pairs={{0,1},{1,0},{2,3},{3,2},{4,5},{5,4},{6,7},{7,6},{8,9},{9,8},{10,11... | collective-permute-start | bytes 6537224 | tf_op jit(solution)/shard_map/ppermute | solution.py:26
  127.5 24.2 %copy-start.27 = (s32[128,2]{0,1:T(2,128)S(1)}, s32[128,2]{0,1:T(2,128)}, u32[]{:S(2)}) copy-start(s32[128,2]{0,1:T(2,128)} %copy-done.26) | copy-start | bytes 3076
  127.6 24.5 %copy-start.2 = (bf16[1,3584,304]{1,2,0:T(8,128)(2,1)S(1)}, bf16[1,3584,304]{1,2,0:T(8,128)(2,1)}, u32[]{:S(2)}) copy-start(bf16[1,3584,304]{1,2,0:T(8,128)(2,1)} %param.18) | copy-start | bytes 6537220
  150.1 28.6 %collective-permute-start.6 = (bf16[192,3584]{1,0:T(8,128)(2,1)}, bf16[192,3584]{1,0:T(8,128)(2,1)S(1)}, u32[]{:S(2)}, u32[]{:S(2)}) collective-permute-start(bf16[192,3584]{1,0:T(8,128)(2,1)} %pad_maximum_fusion.1), channel_id=1, source_target_pairs={{0,6},{2,0},{4,2},{6,4},{1,7},{3,1},{5,3},{7,5},{8,14},{10,8},{12,... | collective-permute-start | bytes 4128776 | tf_op jit(solution)/shard_map/ppermute | solution.py:18
  150.1 30.0 %collective-permute-start.8 = (bf16[192,3584]{1,0:T(8,128)(2,1)}, bf16[192,3584]{1,0:T(8,128)(2,1)}, u32[]{:S(2)}, u32[]{:S(2)}) collective-permute-start(bf16[192,3584]{1,0:T(8,128)(2,1)} %pad_maximum_fusion.1), channel_id=1, source_target_pairs={{0,2},{2,4},{4,6},{6,0},{1,3},{3,5},{5,7},{7,1},{8,10},{10,12},{12... | collective-permute-start | bytes 4128776 | tf_op jit(solution)/shard_map/ppermute | solution.py:18
  169.6 32.9 %copy-start.3 = (bf16[1,3584,304]{1,2,0:T(8,128)(2,1)S(1)}, bf16[1,3584,304]{1,2,0:T(8,128)(2,1)}, u32[]{:S(2)}) copy-start(bf16[1,3584,304]{1,2,0:T(8,128)(2,1)} %param.18) | copy-start | bytes 6537220
  178.6 70.8 %collective-permute-start.14 = (bf16[320,3584]{1,0:T(8,128)(2,1)}, bf16[320,3584]{1,0:T(8,128)(2,1)}, u32[]{:S(2)}, u32[]{:S(2)}) collective-permute-start(bf16[320,3584]{1,0:T(8,128)(2,1)} %bitcast.59), channel_id=1, source_target_pairs={{0,6},{2,0},{4,2},{6,4},{1,7},{3,1},{5,3},{7,5},{8,14},{10,8},{12,... | collective-permute-start | bytes 6881288 | tf_op jit(solution)/shard_map/ppermute | solution.py:18
  180.1 69.4 %collective-permute-start.15 = (bf16[320,3584]{1,0:T(8,128)(2,1)}, bf16[320,3584]{1,0:T(8,128)(2,1)}, u32[]{:S(2)}, u32[]{:S(2)}) collective-permute-start(bf16[320,3584]{1,0:T(8,128)(2,1)} %bitcast.60), channel_id=1, source_target_pairs={{0,2},{2,4},{4,6},{6,0},{1,3},{3,5},{5,7},{7,1},{8,10},{10,12},{12... | collective-permute-start | bytes 6881288 | tf_op jit(solution)/shard_map/ppermute | solution.py:18
  239.2 60.3 %all-to-all-start.2 = ((bf16[16,40,1792]{2,1,0:T(8,128)(2,1)}), bf16[16,40,1792]{2,1,0:T(8,128)(2,1)}, u32[]{:S(2)}, u32[]{:S(2)}) async-start(bf16[16,40,1792]{2,1,0:T(8,128)(2,1)} %bitcast.61), calls=%async_computation.2 | async-start | bytes 4587520 | tf_op jit(solution)/shard_map/all_to_all | solution.py:30
  252.8 23.9 %collective-permute-start.16 = (bf16[320,1792]{1,0:T(8,128)(2,1)}, bf16[320,1792]{1,0:T(8,128)(2,1)S(1)}, u32[]{:S(2)}, u32[]{:S(2)}) collective-permute-start(bf16[320,1792]{1,0:T(8,128)(2,1)} %get-tuple-element.81), channel_id=1, source_target_pairs={{0,2},{2,4},{4,6},{6,0},{1,3},{3,5},{5,7},{7,1},{8,10},{10,12},{12... | collective-permute-start | bytes 3440648 | tf_op jit(solution)/shard_map/ppermute | solution.py:22
  253.7 23.0 %collective-permute-start.17 = (bf16[320,1792]{1,0:T(8,128)(2,1)}, bf16[320,1792]{1,0:T(8,128)(2,1)}, u32[]{:S(2)}, u32[]{:S(2)}) collective-permute-start(bf16[320,1792]{1,0:T(8,128)(2,1)} %get-tuple-element.80), channel_id=1, source_target_pairs={{0,6},{2,0},{4,2},{6,4},{1,7},{3,1},{5,3},{7,5},{8,14},{10,8},{12,... | collective-permute-start | bytes 3440648 | tf_op jit(solution)/shard_map/ppermute | solution.py:22
  276.7 21.7 %copy-start.16 = (bf16[320,1792]{1,0:T(8,128)(2,1)}, bf16[320,1792]{1,0:T(8,128)(2,1)S(1)}, u32[]{:S(2)}) copy-start(bf16[320,1792]{1,0:T(8,128)(2,1)S(1)} %collective-permute-done.16) | copy-start | bytes 3440644
  276.7 22.8 %collective-permute-start.19 = (bf16[128,3584]{1,0:T(8,128)(2,1)}, bf16[128,3584]{1,0:T(8,128)(2,1)S(1)}, u32[]{:S(2)}, u32[]{:S(2)}) collective-permute-start(bf16[128,3584]{1,0:T(8,128)(2,1)} %get-tuple-element.51), channel_id=1, source_target_pairs={{0,6},{2,0},{4,2},{6,4},{1,7},{3,1},{5,3},{7,5},{8,14},{10,8},{12,... | collective-permute-start | bytes 2752520 | tf_op jit(solution)/shard_map/ppermute | solution.py:22
  279.1 20.4 %collective-permute-start.18 = (bf16[128,3584]{1,0:T(8,128)(2,1)}, bf16[128,3584]{1,0:T(8,128)(2,1)}, u32[]{:S(2)}, u32[]{:S(2)}) collective-permute-start(bf16[128,3584]{1,0:T(8,128)(2,1)} %get-tuple-element.50), channel_id=1, source_target_pairs={{0,2},{2,4},{4,6},{6,0},{1,3},{3,5},{5,7},{7,1},{8,10},{10,12},{12... | collective-permute-start | bytes 2752520 | tf_op jit(solution)/shard_map/ppermute | solution.py:22
  303.0 21.7 %collective-permute-start.20 = (bf16[320,1792]{1,0:T(8,128)(2,1)}, bf16[320,1792]{1,0:T(8,128)(2,1)}, u32[]{:S(2)}, u32[]{:S(2)}) collective-permute-start(bf16[320,1792]{1,0:T(8,128)(2,1)} %get-tuple-element.78), channel_id=1, source_target_pairs={{0,2},{2,4},{4,6},{6,0},{1,3},{3,5},{5,7},{7,1},{8,10},{10,12},{12... | collective-permute-start | bytes 3440648 | tf_op jit(solution)/shard_map/ppermute | solution.py:22
  303.1 21.6 %collective-permute-start.21 = (bf16[320,1792]{1,0:T(8,128)(2,1)}, bf16[320,1792]{1,0:T(8,128)(2,1)}, u32[]{:S(2)}, u32[]{:S(2)}) collective-permute-start(bf16[320,1792]{1,0:T(8,128)(2,1)} %get-tuple-element.79), channel_id=1, source_target_pairs={{0,6},{2,0},{4,2},{6,4},{1,7},{3,1},{5,3},{7,5},{8,14},{10,8},{12,... | collective-permute-start | bytes 3440648 | tf_op jit(solution)/shard_map/ppermute | solution.py:22
  307.2 12.9 %all-to-all-start.3 = ((f32[16,1,80]{2,1,0:T(1,128)}), f32[16,1,80]{2,1,0:T(1,128)S(1)}, u32[]{:S(2)}, u32[]{:S(2)}) async-start(f32[16,1,80]{2,1,0:T(1,128)} %bitcast.23), calls=%async_computation.3 | async-start | bytes 16384 | tf_op jit(solution)/shard_map/all_to_all | solution.py:30
  321.4 17.8 %collective-permute-start.22 = (f32[16,20]{1,0:T(8,128)S(1)}, f32[16,20]{1,0:T(8,128)S(1)}, u32[]{:S(2)}, u32[]{:S(2)}) collective-permute-start(f32[16,20]{1,0:T(8,128)S(1)} %bitcast.65), channel_id=1, source_target_pairs={{0,2},{2,4},{4,6},{6,0},{1,3},{3,5},{5,7},{7,1},{8,10},{10,12},{12... | collective-permute-start | bytes 3848 | tf_op jit(solution)/shard_map/ppermute | solution.py:22
  321.5 17.8 %collective-permute-start.23 = (f32[16,20]{1,0:T(8,128)S(1)}, f32[16,20]{1,0:T(8,128)S(1)}, u32[]{:S(2)}, u32[]{:S(2)}) collective-permute-start(f32[16,20]{1,0:T(8,128)S(1)} %bitcast.64), channel_id=1, source_target_pairs={{0,4},{2,6},{4,0},{6,2},{1,5},{3,7},{5,1},{7,3},{8,12},{10,14},{12... | collective-permute-start | bytes 3848 | tf_op jit(solution)/shard_map/ppermute | solution.py:22
  324.2 15.1 %collective-permute-start.24 = (f32[16,20]{1,0:T(8,128)S(1)}, f32[16,20]{1,0:T(8,128)S(1)}, u32[]{:S(2)}, u32[]{:S(2)}) collective-permute-start(f32[16,20]{1,0:T(8,128)S(1)} %bitcast.63), channel_id=1, source_target_pairs={{0,6},{2,0},{4,2},{6,4},{1,7},{3,1},{5,3},{7,5},{8,14},{10,8},{12,... | collective-permute-start | bytes 3848 | tf_op jit(solution)/shard_map/ppermute | solution.py:22
  328.7 25.7 %all-to-all-start.4 = ((bf16[16,40,1792]{2,1,0:T(8,128)(2,1)}), bf16[16,40,1792]{2,1,0:T(8,128)(2,1)S(1)}, u32[]{:S(2)}, u32[]{:S(2)}) async-start(bf16[16,40,1792]{2,1,0:T(8,128)(2,1)} %bitcast.29), calls=%async_computation.4 | async-start | bytes 4587520 | tf_op jit(solution)/shard_map/all_to_all | solution.py:30
  337.2 6.4 %copy-start.25 = (s32[128,2]{0,1:T(2,128)S(1)}, s32[128,2]{0,1:T(2,128)}, u32[]{:S(2)}) copy-start(s32[128,2]{0,1:T(2,128)} %copy-done.24) | copy-start | bytes 3076
  337.2 6.4 %copy-start.29 = (s32[128,2]{0,1:T(2,128)S(1)}, s32[128,2]{0,1:T(2,128)}, u32[]{:S(2)}) copy-start(s32[128,2]{0,1:T(2,128)} %copy-done.28) | copy-start | bytes 3076
  337.2 18.2 %collective-permute-start.25 = (bf16[128,3584]{1,0:T(8,128)(2,1)}, bf16[128,3584]{1,0:T(8,128)(2,1)}, u32[]{:S(2)}, u32[]{:S(2)}) collective-permute-start(bf16[128,3584]{1,0:T(8,128)(2,1)} %fusion.13), channel_id=1, source_target_pairs={{0,4},{2,6},{4,0},{6,2},{1,5},{3,7},{5,1},{7,3},{8,12},{10,14},{12... | collective-permute-start | bytes 2752520 | tf_op jit(solution)/shard_map/ppermute | solution.py:22
  361.2 37.4 %copy-start.11 = (bf16[128,3584]{1,0:T(8,128)(2,1)S(1)}, bf16[128,3584]{1,0:T(8,128)(2,1)}, u32[]{:S(2)}) copy-start(bf16[128,3584]{1,0:T(8,128)(2,1)} %param.12) | copy-start | bytes 2752516
  362.4 30.4 %all-to-all-start.5 = ((f32[128,1,476]{2,1,0:T(1,128)}), f32[128,1,476]{2,1,0:T(1,128)S(1)}, u32[]{:S(2)}, u32[]{:S(2)}) async-start(f32[128,1,476]{2,1,0:T(1,128)} %all_to_all.64), calls=%async_computation.5 | async-start | bytes 524288 | tf_op jit(solution)/shard_map/all_to_all | solution.py:30
  393.9 15.5 %all-to-all-start.6 = ((f32[128,1,476]{2,1,0:T(1,128)}), f32[128,1,476]{2,1,0:T(1,128)S(1)}, u32[]{:S(2)}, u32[]{:S(2)}) async-start(f32[128,1,476]{2,1,0:T(1,128)} %broadcast_in_dim.95), calls=%async_computation.6 | async-start | bytes 524288 | tf_op jit(solution)/shard_map/all_to_all | solution.py:30
  (18 other events, 54.9 us)
